TPU v7x, 256 devices: a whole 4x4x8 slice. The times are simulated.
256 devices in a mesh: ctx: 32 (over z, x_hi, core), head: 8 (over y, x_lo).
Axes of the slice: x: 4 (x_hi: 2, x_lo: 2; x = x_hi * 2 + x_lo), y: 4, z: 8, core: 2. Of those that a mesh axis runs over, the one named last changes fastest.
Arguments:
- queries: bfloat16 [16384, 8192], P(('ctx', 'head')), may hold values from -65 to 65
- key_codes: bfloat16 [16384, 1024], P(('ctx', 'head')), may hold values from -4 to 4
- rotated_value_codes: bfloat16 [16384, 1024], P(('ctx', 'head')), may hold values from -4 to 4
- key_exponents: int32 [16384, 8], P(('ctx', 'head')), may hold values from -2 to 2
- value_block_exponents: int32 [16384, 8], P(('ctx', 'head')), may hold values from -2 to 2
- trace_ids: int32 [16384], P('ctx'), may hold values from 0 to 15, never falling along the last dimension, each value on 1 to 2049 neighbouring positions
Outputs:
- attended: bfloat16 [16384, 8192], P('ctx', 'head')
All inputs are finite; a program needn't handle non-finite values.
Results may differ from a plain program's by a relative error of at most 0.0022.
The roundings to bfloat16 on the way count: a program that leaves them out, or rounds other values in their place, can miss the bound.
Values may be sent and summed in bfloat16 or wider, within the bound.
A program may use at most 64 MiB of HBM per device.

v0:
```python
import math

import jax
import jax.numpy as jnp
from jax import lax
from jax.sharding import PartitionSpec as P

QUERY_HEADS = 64
KEY_VALUE_HEADS = 8
HEAD_SIZE = 128
STEPS = 4


def passed_along(value, axis, steps):
    count = lax.axis_size(axis)
    initial, last = (max(0, -steps), min(count, count - steps))
    return lax.ppermute(value, axis, [(source, source + steps) for source in range(initial, last)])


def count_ones(value_rows, order):
    result = jnp.zeros_like(value_rows)
    for place in range(order.bit_length()):
        result = result + (value_rows >> place & 1)
    return result


def hadamard_signs(order):
    indices = lax.iota(jnp.int32, order)
    parity = count_ones(indices[:, None] & indices[None, :], order) % 2
    return (1 - 2 * parity).astype(jnp.bfloat16)


def dequantize(quantized_codes, scale_exponents):
    rows = quantized_codes.shape[0]
    heads = scale_exponents.shape[1]
    powers = jnp.exp2(scale_exponents.astype(jnp.float32)).astype(jnp.bfloat16)
    scaled = quantized_codes.reshape(rows, heads, HEAD_SIZE) * powers[:, :, None]
    rotated = jnp.dot(
        scaled.reshape(rows * heads, HEAD_SIZE),
        hadamard_signs(HEAD_SIZE),
        preferred_element_type=jnp.float32,
    )
    rotated = rotated * (1.0 / math.sqrt(HEAD_SIZE))
    return rotated.astype(jnp.bfloat16).reshape(rows, heads, HEAD_SIZE)


def attend_tile(state, query_vector, key_block, value_block, allowed):
    running_maximum, weight_total, output_accumulator = state
    scores = jnp.einsum(
        "qhgd,khd->qhgk", query_vector, key_block, preferred_element_type=jnp.float32
    ) * (1.0 / math.sqrt(HEAD_SIZE))
    scores = jnp.where(allowed[:, None, None, :], scores, -jnp.inf)
    newmax = jnp.maximum(running_maximum, jnp.max(scores, axis=-1))
    weights = jnp.exp(scores - newmax[..., None])
    factor = jnp.exp(running_maximum - newmax)
    weight_total = weight_total * factor + jnp.sum(weights, axis=-1)
    output_accumulator = output_accumulator * factor[..., None] + jnp.einsum(
        "qhgk,khd->qhgd",
        weights.astype(jnp.bfloat16),
        value_block,
        preferred_element_type=jnp.float32,
    )
    return (newmax, weight_total, output_accumulator)


def per_device(
    queries, key_codes, rotated_value_codes, key_exponents, value_block_exponents, trace_ids
):
    query_vector, kcodes, vcodes, kexpo, vexpo = (
        lax.all_to_all(queries, "head", split_axis=1, concat_axis=0, tiled=True),
        lax.all_to_all(key_codes, "head", split_axis=1, concat_axis=0, tiled=True),
        lax.all_to_all(rotated_value_codes, "head", split_axis=1, concat_axis=0, tiled=True),
        lax.all_to_all(key_exponents, "head", split_axis=1, concat_axis=0, tiled=True),
        lax.all_to_all(value_block_exponents, "head", split_axis=1, concat_axis=0, tiled=True),
    )
    block = query_vector.shape[0]
    kv_heads = kexpo.shape[1]
    query_groups = QUERY_HEADS // KEY_VALUE_HEADS
    key_rows = dequantize(kcodes, kexpo)
    value_rows = dequantize(vcodes, vexpo)
    query_vector = query_vector.reshape(block, kv_heads, query_groups, HEAD_SIZE)
    position = lax.axis_index("ctx")
    offsets = lax.iota(jnp.int32, block)
    query_pos = position * block + offsets
    state = (
        jnp.full((block, kv_heads, query_groups), -jnp.inf, jnp.float32),
        jnp.zeros((block, kv_heads, query_groups), jnp.float32),
        jnp.zeros((block, kv_heads, query_groups, HEAD_SIZE), jnp.float32),
    )

    def visit(state, key_block, value_block, key_ids, step):
        key_pos = (position - step) * block + offsets
        allowed = (
            (key_pos[None, :] <= query_pos[:, None])
            & (key_pos[None, :] >= 0)
            & (key_ids[None, :] == trace_ids[:, None])
        )
        return attend_tile(state, query_vector, key_block, value_block, allowed)

    state = visit(state, key_rows, value_rows, trace_ids, 0)
    carried = (key_rows, value_rows, trace_ids)
    for step in range(1, STEPS + 1):
        carried = passed_along((carried[0], carried[1], carried[2]), "ctx", 1)
        state = visit(state, carried[0], carried[1], carried[2], step)
    running_maximum, weight_total, output_accumulator = state
    return (
        (output_accumulator / weight_total[..., None])
        .astype(jnp.bfloat16)
        .reshape(block, kv_heads * query_groups * HEAD_SIZE)
    )


def solution(mesh):
    placed = (
        P(("ctx", "head"), None),
        P(("ctx", "head"), None),
        P(("ctx", "head"), None),
        P(("ctx", "head"), None),
        P(("ctx", "head"), None),
        P("ctx"),
    )
    return jax.shard_map(
        per_device, mesh=mesh, in_specs=placed, out_specs=P("ctx", "head"), check_vma=False
    )
```

profile of v0, /device:TPU:103, one launch (start us, length us, event | category | flops | bytes accessed | tf_op | source)
XLA Modules:
  0.0 143.7 jit_solution(3104158669962603197)
XLA Ops:
  0.0 6.3 %collective-permute-start = (s32[512]{0:T(512)}, s32[512]{0:T(512)S(1)}, u32[]{:S(2)}, u32[]{:S(2)}) collective-permute-start(s32[512]{0:T(512)} %param.11), channel_id=1, source_target_pairs={{0,8},{8,16},{16,24},{24,32},{32,40},{40,48},{48,56},{56,64},{64,7... | collective-permute-start | bytes 6152 | tf_op jit(solution)/shard_map/ppermute | solution.py:17
  6.3 5.4 %all-to-all-start.1 = ((s32[64,8,1]{0,2,1:T(1,128)}), s32[64,8,1]{0,2,1:T(1,128)S(1)}, u32[]{:S(2)}, u32[]{:S(2)}) async-start(s32[64,8,1]{0,2,1:T(1,128)} %bitcast.224), calls=%async_computation.1 | async-start | bytes 8192 | tf_op jit(solution)/shard_map/all_to_all | solution.py:73
  14.0 2.3 %copy.155 = bf16[8,8,8,1024]{3,2,0,1:T(8,128)(2,1)} copy(bf16[8,8,8,1024]{3,2,1,0:T(8,128)(2,1)} %bitcast.219) | data formatting | bytes 2097152 | tf_op jit(solution)/shard_map/all_to_all | solution.py:70
  16.3 5.1 %all-to-all-start.4 = ((s32[64,8,1]{0,2,1:T(1,128)}), s32[64,8,1]{0,2,1:T(1,128)S(1)}, u32[]{:S(2)}, u32[]{:S(2)}) async-start(s32[64,8,1]{0,2,1:T(1,128)} %bitcast.225), calls=%async_computation.4 | async-start | bytes 8192 | tf_op jit(solution)/shard_map/all_to_all | solution.py:74
  21.5 3.7 %all-to-all-done.4 = s32[64,8,1]{0,2,1:T(1,128)S(1)} async-done(((s32[64,8,1]{0,2,1:T(1,128)}), s32[64,8,1]{0,2,1:T(1,128)S(1)}, u32[]{:S(2)}, u32[]{:S(2)}) %all-to-all-start.4) | async-done | bytes 2080 | tf_op jit(solution)/shard_map/all_to_all | solution.py:74
  25.2 4.4 %all-to-all-start = ((bf16[64,8,128]{2,0,1:T(8,128)(2,1)}), bf16[64,8,128]{2,0,1:T(8,128)(2,1)S(1)}, u32[]{:S(2)}, u32[]{:S(2)}) async-start(bf16[64,8,128]{2,0,1:T(8,128)(2,1)} %copy_bitcast_fusion.2), calls=%async_computation | async-start | bytes 262144 | tf_op jit(solution)/shard_map/all_to_all | solution.py:71
  29.7 4.5 %all-to-all-done = bf16[64,8,128]{2,0,1:T(8,128)(2,1)S(1)} async-done(((bf16[64,8,128]{2,0,1:T(8,128)(2,1)}), bf16[64,8,128]{2,0,1:T(8,128)(2,1)S(1)}, u32[]{:S(2)}, u32[]{:S(2)}) %all-to-all-start) | async-done | bytes 131104 | tf_op jit(solution)/shard_map/all_to_all | solution.py:71
  34.2 4.3 %all-to-all-start.3 = ((bf16[64,8,128]{2,0,1:T(8,128)(2,1)}), bf16[64,8,128]{2,0,1:T(8,128)(2,1)S(1)}, u32[]{:S(2)}, u32[]{:S(2)}) async-start(bf16[64,8,128]{2,0,1:T(8,128)(2,1)} %copy_bitcast_fusion.1), calls=%async_computation.3 | async-start | bytes 262144 | tf_op jit(solution)/shard_map/all_to_all | solution.py:72
  38.9 5.3 %collective-permute-start.1 = (bf16[512,1,128]{2,0,1:T(8,128)(2,1)S(1)}, bf16[512,1,128]{2,0,1:T(8,128)(2,1)S(1)}, u32[]{:S(2)}, u32[]{:S(2)}) collective-permute-start(bf16[512,1,128]{2,0,1:T(8,128)(2,1)S(1)} %bitcast.221), channel_id=1, source_target_pairs={{0,8},{8,16},{16,24},{24,32},{32,40},{40,48},{48,56},{56,64},{64,7... | collective-permute-start | bytes 393224 | tf_op jit(solution)/shard_map/ppermute | solution.py:17
  44.2 5.2 %all-to-all-start.2 = ((bf16[64,8,1024]{2,0,1:T(8,128)(2,1)}), bf16[64,8,1024]{2,0,1:T(8,128)(2,1)S(1)}, u32[]{:S(2)}, u32[]{:S(2)}) async-start(bf16[64,8,1024]{2,0,1:T(8,128)(2,1)} %bitcast.212), calls=%async_computation.2 | async-start | bytes 2097152 | tf_op jit(solution)/shard_map/all_to_all | solution.py:70
  49.8 4.6 %collective-permute-start.2 = (bf16[512,1,128]{2,0,1:T(8,128)(2,1)S(1)}, bf16[512,1,128]{2,0,1:T(8,128)(2,1)S(1)}, u32[]{:S(2)}, u32[]{:S(2)}) collective-permute-start(bf16[512,1,128]{2,0,1:T(8,128)(2,1)S(1)} %bitcast.226), channel_id=1, source_target_pairs={{0,8},{8,16},{16,24},{24,32},{32,40},{40,48},{48,56},{56,64},{64,7... | collective-permute-start | bytes 393224 | tf_op jit(solution)/shard_map/ppermute | solution.py:17
  54.4 1.9 %collective-permute-start.3 = (s32[512]{0:T(512)S(1)}, s32[512]{0:T(512)S(1)}, u32[]{:S(2)}, u32[]{:S(2)}) collective-permute-start(s32[512]{0:T(512)S(1)} %collective-permute-done), channel_id=1, source_target_pairs={{0,8},{8,16},{16,24},{24,32},{32,40},{40,48},{48,56},{56,64},{64,7... | collective-permute-start | bytes 6152 | tf_op jit(solution)/shard_map/ppermute | solution.py:17
  57.5 7.5 %collective-permute-start.6 = (s32[512]{0:T(512)S(1)}, s32[512]{0:T(512)S(1)}, u32[]{:S(2)}, u32[]{:S(2)}) collective-permute-start(s32[512]{0:T(512)S(1)} %collective-permute-done.3), channel_id=1, source_target_pairs={{0,8},{8,16},{16,24},{24,32},{32,40},{40,48},{48,56},{56,64},{64,7... | collective-permute-start | bytes 6152 | tf_op jit(solution)/shard_map/ppermute | solution.py:17
  65.0 3.9 %collective-permute-start.4 = (bf16[512,1,128]{2,0,1:T(8,128)(2,1)S(1)}, bf16[512,1,128]{2,0,1:T(8,128)(2,1)S(1)}, u32[]{:S(2)}, u32[]{:S(2)}) collective-permute-start(bf16[512,1,128]{2,0,1:T(8,128)(2,1)S(1)} %collective-permute-done.1), channel_id=1, source_target_pairs={{0,8},{8,16},{16,24},{24,32},{32,40},{40,48},{48,56},{56,64},{64,7... | collective-permute-start | bytes 393224 | tf_op jit(solution)/shard_map/ppermute | solution.py:17
  68.9 5.9 %collective-permute-start.5 = (bf16[512,1,128]{2,0,1:T(8,128)(2,1)S(1)}, bf16[512,1,128]{2,0,1:T(8,128)(2,1)S(1)}, u32[]{:S(2)}, u32[]{:S(2)}) collective-permute-start(bf16[512,1,128]{2,0,1:T(8,128)(2,1)S(1)} %collective-permute-done.2), channel_id=1, source_target_pairs={{0,8},{8,16},{16,24},{24,32},{32,40},{40,48},{48,56},{56,64},{64,7... | collective-permute-start | bytes 393224 | tf_op jit(solution)/shard_map/ppermute | solution.py:17
  74.8 1.9 %collective-permute-start.9 = (s32[512]{0:T(512)S(1)}, s32[512]{0:T(512)S(1)}, u32[]{:S(2)}, u32[]{:S(2)}) collective-permute-start(s32[512]{0:T(512)S(1)} %collective-permute-done.6), channel_id=1, source_target_pairs={{0,8},{8,16},{16,24},{24,32},{32,40},{40,48},{48,56},{56,64},{64,7... | collective-permute-start | bytes 6152 | tf_op jit(solution)/shard_map/ppermute | solution.py:17
  76.8 2.0 %collective-permute-start.7 = (bf16[512,1,128]{2,0,1:T(8,128)(2,1)S(1)}, bf16[512,1,128]{2,0,1:T(8,128)(2,1)S(1)}, u32[]{:S(2)}, u32[]{:S(2)}) collective-permute-start(bf16[512,1,128]{2,0,1:T(8,128)(2,1)S(1)} %collective-permute-done.4), channel_id=1, source_target_pairs={{0,8},{8,16},{16,24},{24,32},{32,40},{40,48},{48,56},{56,64},{64,7... | collective-permute-start | bytes 393224 | tf_op jit(solution)/shard_map/ppermute | solution.py:17
  78.8 5.9 %collective-permute-start.8 = (bf16[512,1,128]{2,0,1:T(8,128)(2,1)S(1)}, bf16[512,1,128]{2,0,1:T(8,128)(2,1)}, u32[]{:S(2)}, u32[]{:S(2)}) collective-permute-start(bf16[512,1,128]{2,0,1:T(8,128)(2,1)S(1)} %collective-permute-done.5), channel_id=1, source_target_pairs={{0,8},{8,16},{16,24},{24,32},{32,40},{40,48},{48,56},{56,64},{64,7... | collective-permute-start | bytes 393224 | tf_op jit(solution)/shard_map/ppermute | solution.py:17
  84.7 2.7 %compare_and_fusion.3 = (pred[512,512]{0,1:T(8,128)(4,1)S(1)}, pred[512,512]{0,1:T(8,128)(4,1)S(1)}, pred[512,512]{0,1:T(8,128)(4,1)S(1)}, pred[512,512]{0,1:T(8,128)(4,1)S(1)}, pred[512,512]{0,1:T(8,128)(4,1)S(1)}) fusion(s32[512]{0:T(512)} %param.11, s32[512]{0:T(512)S(1)} %iota_add_fusion.4, s32[512]{0:T(512)S(1)} %collective-permute-done, ...), kind=kLoop, calls=%fused_computation.59 | loop fusion | flops 5242880 | bytes 1333760 | tf_op jit(solution)/shard_map/and | solution.py:94
  87.4 2.0 %collective-permute-start.10 = (bf16[512,1,128]{2,0,1:T(8,128)(2,1)S(1)}, bf16[512,1,128]{2,0,1:T(8,128)(2,1)S(1)}, u32[]{:S(2)}, u32[]{:S(2)}) collective-permute-start(bf16[512,1,128]{2,0,1:T(8,128)(2,1)S(1)} %collective-permute-done.7), channel_id=1, source_target_pairs={{0,8},{8,16},{16,24},{24,32},{32,40},{40,48},{48,56},{56,64},{64,7... | collective-permute-start | bytes 393224 | tf_op jit(solution)/shard_map/ppermute | solution.py:17
  89.4 5.4 %collective-permute-start.11 = (bf16[512,1,128]{2,0,1:T(8,128)(2,1)}, bf16[512,1,128]{2,0,1:T(8,128)(2,1)}, u32[]{:S(2)}, u32[]{:S(2)}) collective-permute-start(bf16[512,1,128]{2,0,1:T(8,128)(2,1)} %collective-permute-done.8), channel_id=1, source_target_pairs={{0,8},{8,16},{16,24},{24,32},{32,40},{40,48},{48,56},{56,64},{64,7... | collective-permute-start | bytes 393224 | tf_op jit(solution)/shard_map/ppermute | solution.py:17
  95.1 1.8 %fusion.10 = (f32[512,8]{0,1:T(8,128)S(1)}, f32[512,512,8]{1,0,2:T(8,128)S(1)}) fusion(pred[512,512]{0,1:T(8,128)(4,1)S(1)} %get-tuple-element.19, bf16[512,8,128]{2,1,0:T(8,128)(2,1)S(1)} %bitcast.213, bf16[512,128]{1,0:T(8,128)(2,1)S(1)} %fusion.41), kind=kOutput, calls=%fused_computation.20 | convolution fusion | flops 543158272 | bytes 9846784 | tf_op jit(solution)/shard_map/qhgd,khd->qhgk/dot_general | solution.py:49
  97.0 3.9 %fusion.20 = f32[128,512,8]{1,0,2:T(8,128)} fusion(f32[512,512,8]{1,0,2:T(8,128)S(1)} %get-tuple-element.27, f32[512,8]{0,1:T(8,128)S(1)} %get-tuple-element.26, pred[512,512]{0,1:T(8,128)(4,1)S(1)} %get-tuple-element.19, bf16[512,128]{1,0:T(8,128)(2,1)S(1)} %copy-done.3), kind=kOutput, calls=%fused_computation.30 | convolution fusion | flops 545259520 | bytes 10895360 | tf_op jit(solution)/shard_map/qhgk,khd->qhgd/dot_general | solution.py:57
  102.7 1.8 %fusion.12 = (f32[512,8]{0,1:T(8,128)S(1)}, f32[512,512,8]{1,0,2:T(8,128)S(1)}) fusion(pred[512,512]{0,1:T(8,128)(4,1)S(1)} %get-tuple-element.16, bf16[512,8,128]{2,1,0:T(8,128)(2,1)S(1)} %bitcast.215, bf16[512,1,128]{2,0,1:T(8,128)(2,1)S(1)} %collective-permute-done.4), kind=kOutput, calls=%fused_computation.22 | convolution fusion | flops 543158272 | bytes 9846784 | tf_op jit(solution)/shard_map/qhgd,khd->qhgk/dot_general | solution.py:49
  104.5 4.8 %fusion.11 = (f32[512,8]{0,1:T(8,128)S(1)}, f32[512,512,8]{1,0,2:T(8,128)}) fusion(pred[512,512]{0,1:T(8,128)(4,1)S(1)} %get-tuple-element.15, bf16[512,8,128]{2,1,0:T(8,128)(2,1)S(1)} %bitcast.216, bf16[512,1,128]{2,0,1:T(8,128)(2,1)S(1)} %collective-permute-done.1), kind=kOutput, calls=%fused_computation.21 | convolution fusion | flops 543158272 | bytes 9846784 | tf_op jit(solution)/shard_map/qhgd,khd->qhgk/dot_general | solution.py:49
  109.3 1.8 %fusion.14 = (f32[512,8]{0,1:T(8,128)S(1)}, f32[512,512,8]{1,0,2:T(8,128)S(1)}) fusion(pred[512,512]{0,1:T(8,128)(4,1)S(1)} %get-tuple-element.18, bf16[512,8,128]{2,1,0:T(8,128)(2,1)S(1)} %bitcast.217, bf16[512,1,128]{2,0,1:T(8,128)(2,1)S(1)} %collective-permute-done.10), kind=kOutput, calls=%fused_computation.24 | convolution fusion | flops 543158272 | bytes 9846784 | tf_op jit(solution)/shard_map/qhgd,khd->qhgk/dot_general | solution.py:49
  111.1 7.6 %fusion = (f32[512,8]{0,1:T(8,128)S(1)}, f32[512,8]{0,1:T(8,128)S(1)}) fusion(f32[512,512,8]{1,0,2:T(8,128)} %copy-done.1, f32[512,8]{0,1:T(8,128)S(1)} %get-tuple-element.26, pred[512,512]{0,1:T(8,128)(4,1)S(1)} %get-tuple-element.19, f32[512,8]{0,1:T(8,128)S(1)} %get-tuple-element.13, f32[512,512,8]{1,0,2:T(8,128)} %get-tuple-element.29, ...), kind=kLoop, calls=%fused_computation.10 | loop fusion | flops 16769024 | bytes 17367040 | tf_op jit(solution)/shard_map/reduce_sum | solution.py:56
  120.5 3.7 %fusion.4 = (f32[512,8]{0,1:T(8,128)S(1)}, f32[512,8]{0,1:T(8,128)S(1)}) fusion(f32[512,512,8]{1,0,2:T(8,128)S(1)} %get-tuple-element.25, f32[512,8]{0,1:T(8,128)S(1)} %get-tuple-element.12, pred[512,512]{0,1:T(8,128)(4,1)S(1)} %get-tuple-element.16, f32[512,8]{0,1:T(8,128)S(1)} %get-tuple-element.11, f32[512,512,8]{1,0,2:T(8,128)S(1)} %get-tuple-element.23, ...), kind=kLoop, calls=%fused_computation.14 | loop fusion | flops 16769024 | bytes 17367040 | tf_op jit(solution)/shard_map/reduce_sum | solution.py:56
  124.2 7.0 %fusion.22 = f32[128,512,8]{1,0,2:T(8,128)} fusion(f32[512,512,8]{1,0,2:T(8,128)} %get-tuple-element.29, f32[512,8]{0,1:T(8,128)S(1)} %get-tuple-element.13, pred[512,512]{0,1:T(8,128)(4,1)S(1)} %get-tuple-element.15, bf16[512,1,128]{2,0,1:T(8,128)(2,1)S(1)} %collective-permute-done.2), kind=kOutput, calls=%fused_computation.31 | convolution fusion | flops 545259520 | bytes 10895360 | tf_op jit(solution)/shard_map/qhgk,khd->qhgd/dot_general | solution.py:57
  131.2 3.7 %fusion.24 = f32[128,512,8]{1,0,2:T(8,128)} fusion(f32[512,512,8]{1,0,2:T(8,128)S(1)} %get-tuple-element.25, f32[512,8]{0,1:T(8,128)S(1)} %get-tuple-element.12, pred[512,512]{0,1:T(8,128)(4,1)S(1)} %get-tuple-element.16, bf16[512,1,128]{2,0,1:T(8,128)(2,1)S(1)} %collective-permute-done.5), kind=kOutput, calls=%fused_computation.32 | convolution fusion | flops 545259520 | bytes 10895360 | tf_op jit(solution)/shard_map/qhgk,khd->qhgd/dot_general | solution.py:57
  135.0 3.5 %fusion.26 = f32[128,512,8]{1,0,2:T(8,128)S(1)} fusion(f32[512,512,8]{1,0,2:T(8,128)S(1)} %get-tuple-element.23, f32[512,8]{0,1:T(8,128)S(1)} %get-tuple-element.11, pred[512,512]{0,1:T(8,128)(4,1)S(1)} %get-tuple-element.17, bf16[512,1,128]{2,0,1:T(8,128)(2,1)} %collective-permute-done.8), kind=kOutput, calls=%fused_computation.33 | convolution fusion | flops 545259520 | bytes 10895360 | tf_op jit(solution)/shard_map/qhgk,khd->qhgd/dot_general | solution.py:57
  138.5 3.8 %fusion.36 = bf16[1,128,512,8]{2,1,3,0:T(8,128)(2,1)S(1)} fusion(f32[128,512,8]{1,0,2:T(8,128)S(1)} %fusion.26, f32[128,512,8]{1,0,2:T(8,128)S(1)} %copy-done.6, f32[128,512,8]{1,0,2:T(8,128)S(1)} %copy-done.5, f32[128,512,8]{1,0,2:T(8,128)S(1)} %copy-done.4, f32[512,8]{0,1:T(8,128)S(1)} %get-tuple-element.5, f32[512,8]{0,1:T(8,128)S(1)} %get-tuple-element.9, ...), kind=kOutput, calls=%fused_computation.42 | convolution fusion | flops 551026688 | bytes 18333696 | tf_op jit(solution)/shard_map/qhgk,khd->qhgd/dot_general | solution.py:57
  (55 shorter events, 9.6 us)
Async XLA Ops:
  0.0 11.7 %copy-start = (bf16[64,1024]{1,0:T(8,128)(2,1)S(1)}, bf16[64,1024]{1,0:T(8,128)(2,1)}, u32[]{:S(2)}) copy-start(bf16[64,1024]{1,0:T(8,128)(2,1)} %param.7) | copy-start | bytes 393220
  0.0 54.4 %collective-permute-start = (s32[512]{0:T(512)}, s32[512]{0:T(512)S(1)}, u32[]{:S(2)}, u32[]{:S(2)}) collective-permute-start(s32[512]{0:T(512)} %param.11), channel_id=1, source_target_pairs={{0,8},{8,16},{16,24},{24,32},{32,40},{40,48},{48,56},{56,64},{64,7... | collective-permute-start | bytes 6152 | tf_op jit(solution)/shard_map/ppermute | solution.py:17
  6.3 10.0 %all-to-all-start.1 = ((s32[64,8,1]{0,2,1:T(1,128)}), s32[64,8,1]{0,2,1:T(1,128)S(1)}, u32[]{:S(2)}, u32[]{:S(2)}) async-start(s32[64,8,1]{0,2,1:T(1,128)} %bitcast.224), calls=%async_computation.1 | async-start | bytes 8192 | tf_op jit(solution)/shard_map/all_to_all | solution.py:73
  16.3 8.9 %all-to-all-start.4 = ((s32[64,8,1]{0,2,1:T(1,128)}), s32[64,8,1]{0,2,1:T(1,128)S(1)}, u32[]{:S(2)}, u32[]{:S(2)}) async-start(s32[64,8,1]{0,2,1:T(1,128)} %bitcast.225), calls=%async_computation.4 | async-start | bytes 8192 | tf_op jit(solution)/shard_map/all_to_all | solution.py:74
  25.2 9.0 %all-to-all-start = ((bf16[64,8,128]{2,0,1:T(8,128)(2,1)}), bf16[64,8,128]{2,0,1:T(8,128)(2,1)S(1)}, u32[]{:S(2)}, u32[]{:S(2)}) async-start(bf16[64,8,128]{2,0,1:T(8,128)(2,1)} %copy_bitcast_fusion.2), calls=%async_computation | async-start | bytes 262144 | tf_op jit(solution)/shard_map/all_to_all | solution.py:71
  34.2 10.0 %all-to-all-start.3 = ((bf16[64,8,128]{2,0,1:T(8,128)(2,1)}), bf16[64,8,128]{2,0,1:T(8,128)(2,1)S(1)}, u32[]{:S(2)}, u32[]{:S(2)}) async-start(bf16[64,8,128]{2,0,1:T(8,128)(2,1)} %copy_bitcast_fusion.1), calls=%async_computation.3 | async-start | bytes 262144 | tf_op jit(solution)/shard_map/all_to_all | solution.py:72
  38.9 26.1 %collective-permute-start.1 = (bf16[512,1,128]{2,0,1:T(8,128)(2,1)S(1)}, bf16[512,1,128]{2,0,1:T(8,128)(2,1)S(1)}, u32[]{:S(2)}, u32[]{:S(2)}) collective-permute-start(bf16[512,1,128]{2,0,1:T(8,128)(2,1)S(1)} %bitcast.221), channel_id=1, source_target_pairs={{0,8},{8,16},{16,24},{24,32},{32,40},{40,48},{48,56},{56,64},{64,7... | collective-permute-start | bytes 393224 | tf_op jit(solution)/shard_map/ppermute | solution.py:17
  44.2 50.6 %all-to-all-start.2 = ((bf16[64,8,1024]{2,0,1:T(8,128)(2,1)}), bf16[64,8,1024]{2,0,1:T(8,128)(2,1)S(1)}, u32[]{:S(2)}, u32[]{:S(2)}) async-start(bf16[64,8,1024]{2,0,1:T(8,128)(2,1)} %bitcast.212), calls=%async_computation.2 | async-start | bytes 2097152 | tf_op jit(solution)/shard_map/all_to_all | solution.py:70
  49.8 34.9 %copy-start.2 = (bf16[512,128]{1,0:T(8,128)(2,1)}, bf16[512,128]{1,0:T(8,128)(2,1)S(1)}, u32[]{:S(2)}) copy-start(bf16[512,128]{1,0:T(8,128)(2,1)S(1)} %fusion.42) | copy-start | bytes 393220
  49.8 19.0 %collective-permute-start.2 = (bf16[512,1,128]{2,0,1:T(8,128)(2,1)S(1)}, bf16[512,1,128]{2,0,1:T(8,128)(2,1)S(1)}, u32[]{:S(2)}, u32[]{:S(2)}) collective-permute-start(bf16[512,1,128]{2,0,1:T(8,128)(2,1)S(1)} %bitcast.226), channel_id=1, source_target_pairs={{0,8},{8,16},{16,24},{24,32},{32,40},{40,48},{48,56},{56,64},{64,7... | collective-permute-start | bytes 393224 | tf_op jit(solution)/shard_map/ppermute | solution.py:17
  54.4 3.1 %collective-permute-start.3 = (s32[512]{0:T(512)S(1)}, s32[512]{0:T(512)S(1)}, u32[]{:S(2)}, u32[]{:S(2)}) collective-permute-start(s32[512]{0:T(512)S(1)} %collective-permute-done), channel_id=1, source_target_pairs={{0,8},{8,16},{16,24},{24,32},{32,40},{40,48},{48,56},{56,64},{64,7... | collective-permute-start | bytes 6152 | tf_op jit(solution)/shard_map/ppermute | solution.py:17
  57.5 17.3 %collective-permute-start.6 = (s32[512]{0:T(512)S(1)}, s32[512]{0:T(512)S(1)}, u32[]{:S(2)}, u32[]{:S(2)}) collective-permute-start(s32[512]{0:T(512)S(1)} %collective-permute-done.3), channel_id=1, source_target_pairs={{0,8},{8,16},{16,24},{24,32},{32,40},{40,48},{48,56},{56,64},{64,7... | collective-permute-start | bytes 6152 | tf_op jit(solution)/shard_map/ppermute | solution.py:17
  65.0 11.7 %collective-permute-start.4 = (bf16[512,1,128]{2,0,1:T(8,128)(2,1)S(1)}, bf16[512,1,128]{2,0,1:T(8,128)(2,1)S(1)}, u32[]{:S(2)}, u32[]{:S(2)}) collective-permute-start(bf16[512,1,128]{2,0,1:T(8,128)(2,1)S(1)} %collective-permute-done.1), channel_id=1, source_target_pairs={{0,8},{8,16},{16,24},{24,32},{32,40},{40,48},{48,56},{56,64},{64,7... | collective-permute-start | bytes 393224 | tf_op jit(solution)/shard_map/ppermute | solution.py:17
  68.9 9.9 %collective-permute-start.5 = (bf16[512,1,128]{2,0,1:T(8,128)(2,1)S(1)}, bf16[512,1,128]{2,0,1:T(8,128)(2,1)S(1)}, u32[]{:S(2)}, u32[]{:S(2)}) collective-permute-start(bf16[512,1,128]{2,0,1:T(8,128)(2,1)S(1)} %collective-permute-done.2), channel_id=1, source_target_pairs={{0,8},{8,16},{16,24},{24,32},{32,40},{40,48},{48,56},{56,64},{64,7... | collective-permute-start | bytes 393224 | tf_op jit(solution)/shard_map/ppermute | solution.py:17
  74.8 9.9 %collective-permute-start.9 = (s32[512]{0:T(512)S(1)}, s32[512]{0:T(512)S(1)}, u32[]{:S(2)}, u32[]{:S(2)}) collective-permute-start(s32[512]{0:T(512)S(1)} %collective-permute-done.6), channel_id=1, source_target_pairs={{0,8},{8,16},{16,24},{24,32},{32,40},{40,48},{48,56},{56,64},{64,7... | collective-permute-start | bytes 6152 | tf_op jit(solution)/shard_map/ppermute | solution.py:17
  76.8 10.6 %collective-permute-start.7 = (bf16[512,1,128]{2,0,1:T(8,128)(2,1)S(1)}, bf16[512,1,128]{2,0,1:T(8,128)(2,1)S(1)}, u32[]{:S(2)}, u32[]{:S(2)}) collective-permute-start(bf16[512,1,128]{2,0,1:T(8,128)(2,1)S(1)} %collective-permute-done.4), channel_id=1, source_target_pairs={{0,8},{8,16},{16,24},{24,32},{32,40},{40,48},{48,56},{56,64},{64,7... | collective-permute-start | bytes 393224 | tf_op jit(solution)/shard_map/ppermute | solution.py:17
  78.8 10.7 %collective-permute-start.8 = (bf16[512,1,128]{2,0,1:T(8,128)(2,1)S(1)}, bf16[512,1,128]{2,0,1:T(8,128)(2,1)}, u32[]{:S(2)}, u32[]{:S(2)}) collective-permute-start(bf16[512,1,128]{2,0,1:T(8,128)(2,1)S(1)} %collective-permute-done.5), channel_id=1, source_target_pairs={{0,8},{8,16},{16,24},{24,32},{32,40},{40,48},{48,56},{56,64},{64,7... | collective-permute-start | bytes 393224 | tf_op jit(solution)/shard_map/ppermute | solution.py:17
  87.4 21.9 %collective-permute-start.10 = (bf16[512,1,128]{2,0,1:T(8,128)(2,1)S(1)}, bf16[512,1,128]{2,0,1:T(8,128)(2,1)S(1)}, u32[]{:S(2)}, u32[]{:S(2)}) collective-permute-start(bf16[512,1,128]{2,0,1:T(8,128)(2,1)S(1)} %collective-permute-done.7), channel_id=1, source_target_pairs={{0,8},{8,16},{16,24},{24,32},{32,40},{40,48},{48,56},{56,64},{64,7... | collective-permute-start | bytes 393224 | tf_op jit(solution)/shard_map/ppermute | solution.py:17
  89.4 49.1 %collective-permute-start.11 = (bf16[512,1,128]{2,0,1:T(8,128)(2,1)}, bf16[512,1,128]{2,0,1:T(8,128)(2,1)}, u32[]{:S(2)}, u32[]{:S(2)}) collective-permute-start(bf16[512,1,128]{2,0,1:T(8,128)(2,1)} %collective-permute-done.8), channel_id=1, source_target_pairs={{0,8},{8,16},{16,24},{24,32},{32,40},{40,48},{48,56},{56,64},{64,7... | collective-permute-start | bytes 393224 | tf_op jit(solution)/shard_map/ppermute | solution.py:17
  94.9 2.1 %copy-start.3 = (bf16[512,128]{1,0:T(8,128)(2,1)S(1)}, bf16[512,128]{1,0:T(8,128)(2,1)}, u32[]{:S(2)}) copy-start(bf16[512,128]{1,0:T(8,128)(2,1)} %copy-done.2) | copy-start | bytes 393220
  97.0 5.7 %copy-start.1 = (f32[512,512,8]{1,0,2:T(8,128)}, f32[512,512,8]{1,0,2:T(8,128)S(1)}, u32[]{:S(2)}) copy-start(f32[512,512,8]{1,0,2:T(8,128)S(1)} %get-tuple-element.27) | copy-start | bytes 25165828
  135.0 3.5 %copy-start.4 = (f32[128,512,8]{1,0,2:T(8,128)S(1)}, f32[128,512,8]{1,0,2:T(8,128)}, u32[]{:S(2)}) copy-start(f32[128,512,8]{1,0,2:T(8,128)} %fusion.20) | copy-start | bytes 6291460
  135.0 3.5 %copy-start.5 = (f32[128,512,8]{1,0,2:T(8,128)S(1)}, f32[128,512,8]{1,0,2:T(8,128)}, u32[]{:S(2)}) copy-start(f32[128,512,8]{1,0,2:T(8,128)} %fusion.22) | copy-start | bytes 6291460
  135.0 3.5 %copy-start.6 = (f32[128,512,8]{1,0,2:T(8,128)S(1)}, f32[128,512,8]{1,0,2:T(8,128)}, u32[]{:S(2)}) copy-start(f32[128,512,8]{1,0,2:T(8,128)} %fusion.24) | copy-start | bytes 6291460
where the time goes:
time: 145 us; the launch traced here: 144 us
  starting transfers between devices  77 us (53%)
  matrix products  34.4 us (24%)
  other arithmetic  16.1 us (11%)
  waiting for transfers between devices  9.29 us (6%)
  local copies, waits for them, and re-layouts  6.31 us (4%)
    ppermute x12, starting transfers between devices, passed_along(): lax.ppermute(value, axis, [(source, source + steps) for source in range(i...  52.6 us
    dot_general x5, matrix products, attend_tile(): jnp.einsum('qhgk,khd->qhgd', weights.astype(jnp.bfloat16), value_block, p...  21.9 us
    reduce_sum x3, other arithmetic, attend_tile(): weight_total = weight_total * factor + jnp.sum(weights, axis=-1)  13.1 us
    dot_general x5, matrix products, attend_tile(): jnp.einsum('qhgd,khd->qhgk', query_vector, key_block, preferred_element_t...  12 us
    all_to_all x1, starting transfers between devices, per_device(): lax.all_to_all(key_exponents, 'head', split_axis=1, concat_axis=0, tiled=...  5.38 us
    all_to_all x1, starting transfers between devices, per_device(): lax.all_to_all(queries, 'head', split_axis=1, concat_axis=0, tiled=True)  5.18 us
    all_to_all x1, starting transfers between devices, per_device(): lax.all_to_all(value_block_exponents, 'head', split_axis=1, concat_axis=0...  5.14 us
    all_to_all x1, waiting for transfers between devices, per_device(): lax.all_to_all(key_codes, 'head', split_axis=1, concat_axis=0, tiled=True)  4.48 us
  transfers between devices with their start and end apart: 17, of which 3 were waited for; matrix products, arithmetic and copies ran while one was open for 36% of the time, Pallas kernels for 0%

commit v1 on v0

v1 whole, which is shorter than its diff:
```python
import math

import jax
import jax.numpy as jnp
from jax import lax
from jax.experimental import pallas as pl
from jax.experimental.pallas import tpu as pltpu
from jax.sharding import PartitionSpec as P

BLOCK = 512
ROWS = 64
PEERS = 8
GROUP = 8
D = 128
STEPS = 4
N_CTX = 32
SCALE = 1.0 / math.sqrt(D)
LOG2E_SCALE = SCALE * math.log2(math.e)
BIG = -1e30
META = BLOCK + 4 * D
KV_ROWS = META + 16
MESH = pl.DeviceIdType.MESH
F32 = jnp.float32
BF16 = jnp.bfloat16


def iota(shape, dimension):
    return lax.broadcasted_iota(jnp.int32, shape, dimension)


def nt_dot(a, b):
    return lax.dot_general(a, b, (((1,), (1,)), ((), ())), preferred_element_type=F32)


def kernel(
    q_hbm, kc_hbm, vc_hbm, ke_hbm, ve_hbm, ids_hbm, out_ref,
    q_ref, kc_ref, vc_ref, ke_ref, ve_ref, ids_ref,
    kvs, kvr, kvr2, kvb, qb, aug_q, aug_k, s_buf,
    in_sem, kv_send, kv_recv, q_send, q_recv, a_send, a_recv, c_send, c_recv,
):
    c = lax.axis_index("ctx")
    h = lax.axis_index("head")
    core = lax.rem(c, 2)
    hy, hx = h // 2, lax.rem(h, 2)

    def to_peer(r):
        ry, rx = r // 2, r % 2
        return lax.rem(hy + ry, 4) * 2 + lax.rem(hx + rx, 2)

    sibling = c + 1 - 2 * core

    barrier = pltpu.get_barrier_semaphore()
    for r in range(1, PEERS):
        pl.semaphore_signal(barrier, inc=1, device_id=(c, to_peer(r)), device_id_type=MESH)
    pl.semaphore_signal(barrier, inc=1, device_id=(sibling, h), device_id_type=MESH)
    @pl.when(c >= 2)
    def _():
        for j in range(PEERS):
            pl.semaphore_signal(barrier, inc=1, device_id=(c - 2, j), device_id_type=MESH)

    @pl.when(c < N_CTX - 2)
    def _():
        for j in range(PEERS):
            pl.semaphore_signal(barrier, inc=1, device_id=(c + 2, j), device_id_type=MESH)

    @pl.when(c >= 4)
    def _():
        pl.semaphore_signal(barrier, inc=1, device_id=(c - 4, h), device_id_type=MESH)

    @pl.when(c < N_CTX - 4)
    def _():
        pl.semaphore_signal(barrier, inc=1, device_id=(c + 4, h), device_id_type=MESH)

    fetches = [
        pltpu.make_async_copy(source, target, in_sem.at[number])
        for number, (source, target) in enumerate(
            (
                (ke_hbm, ke_ref), (ve_hbm, ve_ref), (kc_hbm, kc_ref), (vc_hbm, vc_ref), (ids_hbm, ids_ref),
                (q_hbm, q_ref),
            )
        )
    ]
    for fetch in fetches:
        fetch.start()

    def q_columns(peer):
        return q_ref.at[:, pl.ds(pl.multiple_of(peer * GROUP * D, GROUP * D), GROUP * D)]

    own_q = pltpu.make_async_copy(q_columns(h), qb.at[h], in_sem.at[6])

    bits = iota((D, D), 0) & iota((D, D), 1)
    bits = bits ^ (bits >> 4)
    bits = bits ^ (bits >> 2)
    bits = bits ^ (bits >> 1)
    signs = (1 - 2 * (bits & 1)).astype(F32).astype(BF16)

    for fetch in fetches[:5]:
        fetch.wait()
    k_powers = jnp.exp2(ke_ref[...].astype(F32)).astype(BF16).astype(F32).T
    v_powers = jnp.exp2(ve_ref[...].astype(F32)).astype(BF16).astype(F32).T
    for j in range(PEERS):
        columns = slice(j * D, (j + 1) * D)
        kvs[j, :, 0:D] = (kc_ref[:, columns].astype(F32) * k_powers[:, j:j + 1]).astype(BF16)
        kvs[j, :, D:2 * D] = (vc_ref[:, columns].astype(F32) * v_powers[:, j:j + 1]).astype(BF16)

    ids = ids_ref[...]
    term = iota((D, BLOCK), 0)
    below = jnp.where(ids < term, 1.0, 0.0).astype(F32).astype(BF16)
    upto = jnp.where(ids <= term, 1.0, 0.0).astype(F32).astype(BF16)
    ones = jnp.ones((16, BLOCK), BF16)
    lo, hi = nt_dot(ones, below), nt_dot(ones, upto)
    lo_part, hi_part = jnp.floor(lo * (1.0 / 16)), jnp.floor(hi * (1.0 / 16))
    row = iota((16, D), 0)
    meta = jnp.where(
        row < 4, lo_part,
        jnp.where(row < 8, lo - 16 * lo_part, jnp.where(row < 12, hi_part, hi - 16 * hi_part)),
    )
    kvb[0, META:KV_ROWS] = meta.astype(BF16)

    pl.semaphore_wait(
        barrier,
        PEERS
        + PEERS * (c >= 2).astype(jnp.int32) + (c >= 4).astype(jnp.int32)
        + PEERS * (c < N_CTX - 2).astype(jnp.int32) + (c < N_CTX - 4).astype(jnp.int32),
    )

    my_rows = pl.ds(pl.multiple_of(h * ROWS, ROWS), ROWS)
    kv_copies = {}
    for r in range(1, PEERS):
        peer = to_peer(r)
        kv_copies[r] = pltpu.make_async_remote_copy(
            src_ref=kvs.at[peer], dst_ref=kvr.at[my_rows],
            send_sem=kv_send.at[r], recv_sem=kv_recv.at[r],
            device_id=(c, peer), device_id_type=MESH,
        )
        kv_copies[r].start()

    after2 = lax.rem(c + 2, N_CTX)
    a_copies = [
        pltpu.make_async_remote_copy(
            src_ref=kvs.at[j], dst_ref=kvr2.at[my_rows],
            send_sem=a_send.at[j], recv_sem=a_recv.at[h],
            device_id=(after2, j), device_id_type=MESH,
        )
        for j in range(PEERS)
    ]
    a_copies.append(
        pltpu.make_async_remote_copy(
            src_ref=kvb.at[0, META:KV_ROWS], dst_ref=kvb.at[2, META:KV_ROWS],
            send_sem=a_send.at[PEERS], recv_sem=a_recv.at[PEERS],
            device_id=(after2, h), device_id_type=MESH,
        )
    )

    @pl.when(c < N_CTX - 2)
    def _():
        for copy in a_copies:
            copy.start()

    def q_copy(r):
        peer = to_peer(r)
        return pltpu.make_async_remote_copy(
            src_ref=q_columns(peer), dst_ref=qb.at[h],
            send_sem=q_send.at[r], recv_sem=q_recv.at[h],
            device_id=(c, peer), device_id_type=MESH,
        )

    q_copies = {r: q_copy(r) for r in range(1, PEERS)}
    fetches[5].wait()
    own_q.start()
    for r in (2, 6, 4):
        q_copies[r].start()
    kvr[my_rows] = kvs[h]

    token = iota((BLOCK, D), 0).astype(F32)
    lane = iota((BLOCK, D), 1)
    inside = (token >= lo[0:1]) & (token < hi[0:1])
    diagonal = (lane >= D - ROWS) & (lax.rem(iota((BLOCK, D), 0), ROWS) == lane - (D - ROWS))
    aug_q[...] = jnp.where(inside | diagonal, 1.0, 0.0).astype(F32).astype(BF16)

    def key_spans(d):
        spans = kvb[d, META:KV_ROWS].astype(F32)
        first = spans[0:1] * 16 + spans[4:5]
        last = spans[8:9] * 16 + spans[12:13]
        member = (token >= first) & (token < last)
        aug_k[d] = jnp.where(member | (lane >= D - ROWS), 0.0, BIG).astype(F32).astype(BF16)

    for r in range(1, PEERS):
        kv_copies[r].wait_recv()

    def rotate(codes, slot):
        keys = jnp.dot(codes[:, 0:D], signs, preferred_element_type=F32) * SCALE
        kvb[slot, 0:BLOCK] = keys.astype(BF16)
        values = (nt_dot(signs, codes[:, D:2 * D]) * SCALE).astype(BF16)
        for part in range(4):
            kvb[slot, BLOCK + part * D:BLOCK + (part + 1) * D] = values[:, part * D:(part + 1) * D]

    def c_copy(source, slot, target):
        return pltpu.make_async_remote_copy(
            src_ref=kvb.at[source], dst_ref=kvb.at[slot],
            send_sem=c_send.at[slot], recv_sem=c_recv.at[slot],
            device_id=(target, h), device_id_type=MESH,
        )

    c_copies = {
        1: c_copy(2 * core, 1, sibling),
        3: c_copy(2 + 2 * core, 3, sibling),
        4: c_copy(0, 4, lax.rem(c + 4, N_CTX)),
    }
    rotate(kvr, 0)

    @pl.when(c < N_CTX - 4)
    def _():
        c_copies[4].start()

    @pl.when(core == 0)
    def _():
        c_copies[1].start()

    for r in (1, 3, 7, 5):
        q_copies[r].start()
    key_spans(0)

    @pl.when(c >= 2)
    def _():
        for j in range(PEERS):
            pltpu.make_async_remote_copy(
                src_ref=kvs.at[0], dst_ref=kvr2.at[j * ROWS:(j + 1) * ROWS],
                send_sem=a_send.at[0], recv_sem=a_recv.at[j],
                device_id=(after2, h), device_id_type=MESH,
            ).wait_recv()
        a_copies[PEERS].wait_recv()
        rotate(kvr2, 2)

    @pl.when(c < 2)
    def _():
        kvb[2] = jnp.zeros((KV_ROWS, D), BF16)

    @pl.when(c < 4)
    def _():
        kvb[4] = jnp.zeros((KV_ROWS, D), BF16)

    @pl.when(core == 0)
    def _():
        c_copies[3].start()

    @pl.when(core == 1)
    def _():
        c_copies[1].start()

    key_spans(2)

    @pl.when(c >= 4)
    def _():
        c_copies[4].wait_recv()

    @pl.when(core == 1)
    def _():
        c_copies[3].start()

    key_spans(4)
    c_copies[1].wait_recv()
    key_spans(1)
    c_copies[3].wait_recv()
    key_spans(3)

    half = BLOCK // 2

    def attend(p, first_keys, last_keys):
        extra = aug_q[pl.ds(pl.multiple_of(p * ROWS, ROWS), ROWS)]
        extra = jnp.concatenate([extra] * (GROUP // 2), axis=0)
        spans = [(0, first_keys)] + [(0, BLOCK)] * 3 + [(last_keys, BLOCK)]

        def queries_of(g):
            heads = [qb[p, :, i * D:(i + 1) * D] for i in range(g * GROUP // 2, (g + 1) * GROUP // 2)]
            return jnp.concatenate([jnp.concatenate(heads, axis=0), extra], axis=1)

        def pieces(d):
            start, stop = spans[d]
            return [(k, g) for g in range(2) for k in range(start, stop, half)]

        def score(d, k, g, top):
            extra_keys = aug_k[d, k:k + half]
            if d == 0:
                column = iota((half, D), 1)
                late = (iota((half, D), 0) + k - p * ROWS > column - (D - ROWS)) & (column >= D - ROWS)
                extra_keys = jnp.where(late, BIG, extra_keys.astype(F32)).astype(BF16)
            keys = jnp.concatenate([kvb[d, k:k + half], extra_keys], axis=1)
            scores = nt_dot(keys, queries_of(g))
            s_buf[d % 2, k:k + half, g * half:(g + 1) * half] = scores
            here = jnp.max(scores.reshape(half // 8, 8, half), axis=0)
            top[g] = here if top[g] is None else jnp.maximum(top[g], here)

        def values_of(d, k):
            parts = [kvb[d, BLOCK + part * D:BLOCK + (part + 1) * D] for part in range(k // D, (k + half) // D)]
            return jnp.concatenate(parts, axis=1)

        top = [None, None]
        for k, g in pieces(0):
            score(0, k, g, top)
        running, total, accum = [None, None], [None, None], [None, None]
        for d in range(STEPS + 1):
            next_top = [None, None]
            now = pieces(d)
            following = pieces(d + 1) if d < STEPS else []
            for slot in range(max(len(now), len(following))):
                if slot < len(following):
                    score(d + 1, *following[slot], next_top)
                if slot >= len(now):
                    continue
                k, g = now[slot]
                if top[g] is not None:
                    newmax = jnp.max(top[g], axis=0, keepdims=True)
                    if d:
                        newmax = jnp.maximum(running[g], newmax)
                        factor = jnp.exp2((running[g] - newmax) * LOG2E_SCALE)
                        total[g] = total[g] * factor
                        accum[g] = accum[g] * factor
                    running[g] = newmax
                    top[g] = None
                scores = s_buf[d % 2, k:k + half, g * half:(g + 1) * half]
                weights = jnp.exp2((scores - running[g]) * LOG2E_SCALE)
                sums = jnp.sum(weights.reshape(half // 8, 8, half), axis=0)
                product = jnp.dot(values_of(d, k), weights.astype(BF16), preferred_element_type=F32)
                total[g] = sums if total[g] is None else total[g] + sums
                accum[g] = product if accum[g] is None else accum[g] + product
            top = next_top
        for g in range(2):
            attended = accum[g] * (1.0 / jnp.sum(total[g], axis=0, keepdims=True))
            attended = attended.T.astype(BF16)
            rows = pl.ds(pl.multiple_of(p * ROWS, ROWS), ROWS)
            for i in range(GROUP // 2):
                column = (g * GROUP // 2 + i) * D
                out_ref[rows, column:column + D] = attended[i * ROWS:(i + 1) * ROWS]

    def body(i, carry):
        turn, rx = lax.rem(i, 4), i // 4
        ry = turn + (turn // 2) * (5 - 2 * turn)
        p = lax.rem(hy + 4 - ry, 4) * 2 + lax.rem(hx + rx, 2)

        @pl.when(i == 0)
        def _():
            own_q.wait()

        @pl.when(i > 0)
        def _():
            pltpu.make_async_remote_copy(
                src_ref=q_columns(h), dst_ref=qb.at[p],
                send_sem=q_send.at[0], recv_sem=q_recv.at[p],
                device_id=(c, lax.rem(h + 1, PEERS)), device_id_type=MESH,
            ).wait_recv()

        @pl.when(p < PEERS // 2)
        def _():
            attend(p, half, 0)

        @pl.when(p >= PEERS // 2)
        def _():
            attend(p, BLOCK, half)

        return carry

    lax.fori_loop(0, PEERS, body, 0)

    for r in range(1, PEERS):
        kv_copies[r].wait_send()
        q_copies[r].wait_send()
    for step in (1, 3):
        c_copies[step].wait_send()

    @pl.when(c < N_CTX - 2)
    def _():
        for copy in a_copies:
            copy.wait_send()

    @pl.when(c < N_CTX - 4)
    def _():
        c_copies[4].wait_send()


def per_device(queries, key_codes, value_codes, key_exponents, value_exponents, trace_ids):
    hbm = pl.BlockSpec(memory_space=pl.ANY)
    dma = pltpu.SemaphoreType.DMA
    return pl.pallas_call(
        kernel,
        out_shape=jax.ShapeDtypeStruct((BLOCK, GROUP * D), BF16),
        in_specs=[hbm] * 6,
        out_specs=pl.BlockSpec(memory_space=pltpu.VMEM),
        scratch_shapes=[
            pltpu.VMEM((ROWS, PEERS * GROUP * D), BF16),
            pltpu.VMEM((ROWS, PEERS * D), BF16),
            pltpu.VMEM((ROWS, PEERS * D), BF16),
            pltpu.VMEM((PEERS, ROWS), jnp.int32),
            pltpu.VMEM((PEERS, ROWS), jnp.int32),
            pltpu.VMEM((1, BLOCK), jnp.int32),
            pltpu.VMEM((PEERS, ROWS, 2 * D), BF16),
            pltpu.VMEM((BLOCK, 2 * D), BF16),
            pltpu.VMEM((BLOCK, 2 * D), BF16),
            pltpu.VMEM((STEPS + 1, KV_ROWS, D), BF16),
            pltpu.VMEM((PEERS, ROWS, GROUP * D), BF16),
            pltpu.VMEM((BLOCK, D), BF16),
            pltpu.VMEM((STEPS + 1, BLOCK, D), BF16),
            pltpu.VMEM((2, BLOCK, BLOCK), F32),
            dma((7,)), dma((PEERS,)), dma((PEERS,)), dma((PEERS,)), dma((PEERS,)),
            dma((PEERS + 1,)), dma((PEERS + 1,)), dma((STEPS + 1,)), dma((STEPS + 1,)),
        ],
        compiler_params=pltpu.CompilerParams(
            collective_id=0, has_side_effects=True, vmem_limit_bytes=62 * 1024 * 1024
        ),
        cost_estimate=pl.CostEstimate(flops=9_000_000_000, bytes_accessed=4_000_000, transcendentals=8_700_000),
    )(
        queries, key_codes, value_codes, key_exponents.T, value_exponents.T, trace_ids.reshape(1, BLOCK)
    )


def solution(mesh):
    placed = (
        P(("ctx", "head"), None),
        P(("ctx", "head"), None),
        P(("ctx", "head"), None),
        P(("ctx", "head"), None),
        P(("ctx", "head"), None),
        P("ctx"),
    )
    return jax.shard_map(
        per_device, mesh=mesh, in_specs=placed, out_specs=P("ctx", "head"), check_vma=False
    )
```

time: 145 us -> 39.8 us (0.27)
  the two profiles are of different devices: /device:TPU:103 before, /device:TPU:224 now
where the time goes in v1:
time: 39.8 us; the launch traced here: 39.6 us
  Pallas kernels  37.3 us (94%)
  local copies, waits for them, and re-layouts  2.26 us (6%)
    pallas_call x1, Pallas kernels, per_device(): pl.pallas_call(kernel, out_shape=jax.ShapeDtypeStruct((BLOCK, GROUP * D),...  37.3 us
    unnamed x1, local copies, waits for them, and re-layouts  2.26 us

profile of v1, /device:TPU:224, one launch (start us, length us, event | category | flops | bytes accessed | tf_op | source)
XLA Modules:
  0.0 39.6 jit_solution(8698655709142632384)
XLA Ops:
  0.0 37.3 %shard_map.64 = bf16[512,1024]{1,0:T(8,128)(2,1)} custom-call(bf16[64,8192]{1,0:T(8,128)(2,1)} %q_hbm.1, bf16[64,1024]{1,0:T(8,128)(2,1)} %kc_hbm.1, bf16[64,1024]{1,0:T(8,128)(2,1)} %vc_hbm.1, s32[8,64]{1,0:T(8,128)} %bitcast.3, s32[8,64]{1,0:T(8,128)} %bitcast.4, s32[1,512]{1,0:T(1,128)} %bitcast.5), custom_call_target="tpu_custom_call" | custom-call | flops 8999999488 | bytes 4000000 | tf_op jit(solution)/shard_map/pallas_call | solution.py:384
  37.4 2.3 %copy.8 = bf16[512,1024]{1,0:T(8,128)(2,1)} copy(bf16[512,1024]{1,0:T(8,128)(2,1)} %shard_map.64) | data formatting | bytes 2097152

commit v2 on v1

--- a/solution.py
+++ b/solution.py
@@ -35,7 +35,7 @@
 def kernel(
     q_hbm, kc_hbm, vc_hbm, ke_hbm, ve_hbm, ids_hbm, out_ref,
     q_ref, kc_ref, vc_ref, ke_ref, ve_ref, ids_ref,
-    kvs, kvr, kvr2, kvb, qb, aug_q, aug_k, s_buf,
+    kvs, kvr, kvr2, kvb, qb, aug_q, aug_k, s_buf, top_s, m_s, l_s, o_s,
     in_sem, kv_send, kv_recv, q_send, q_recv, a_send, a_recv, c_send, c_recv,
 ):
     c = lax.axis_index("ctx")
@@ -43,15 +43,22 @@
     core = lax.rem(c, 2)
     hy, hx = h // 2, lax.rem(h, 2)
 
-    def to_peer(r):
-        ry, rx = r // 2, r % 2
-        return lax.rem(hy + ry, 4) * 2 + lax.rem(hx + rx, 2)
+    y_low = lax.rem(hy, 2)
+
+    def partner(turn, n):
+        base = lax.rem(hy - y_low + 2 * turn, 4)
+        flip = lax.rem(turn + n, 2)
+        y = base + y_low + flip * (1 - 2 * y_low)
+        return y * 2 + lax.rem(hx + n // 2, 2)
+
+    others = [(turn, n) for turn in range(2) for n in range(4)][1:]
+    peers = {r: partner(*others[r - 1]) for r in range(1, PEERS)}
 
     sibling = c + 1 - 2 * core
 
     barrier = pltpu.get_barrier_semaphore()
     for r in range(1, PEERS):
-        pl.semaphore_signal(barrier, inc=1, device_id=(c, to_peer(r)), device_id_type=MESH)
+        pl.semaphore_signal(barrier, inc=1, device_id=(c, peers[r]), device_id_type=MESH)
     pl.semaphore_signal(barrier, inc=1, device_id=(sibling, h), device_id_type=MESH)
     @pl.when(c >= 2)
     def _():
@@ -127,7 +134,7 @@
     my_rows = pl.ds(pl.multiple_of(h * ROWS, ROWS), ROWS)
     kv_copies = {}
     for r in range(1, PEERS):
-        peer = to_peer(r)
+        peer = peers[r]
         kv_copies[r] = pltpu.make_async_remote_copy(
             src_ref=kvs.at[peer], dst_ref=kvr.at[my_rows],
             send_sem=kv_send.at[r], recv_sem=kv_recv.at[r],
@@ -158,7 +165,7 @@
             copy.start()
 
     def q_copy(r):
-        peer = to_peer(r)
+        peer = peers[r]
         return pltpu.make_async_remote_copy(
             src_ref=q_columns(peer), dst_ref=qb.at[h],
             send_sem=q_send.at[r], recv_sem=q_recv.at[h],
@@ -168,7 +175,7 @@
     q_copies = {r: q_copy(r) for r in range(1, PEERS)}
     fetches[5].wait()
     own_q.start()
-    for r in (2, 6, 4):
+    for r in (1, 4, 5):
         q_copies[r].start()
     kvr[my_rows] = kvs[h]
 
@@ -217,7 +224,7 @@
     def _():
         c_copies[1].start()
 
-    for r in (1, 3, 7, 5):
+    for r in (2, 3, 6, 7):
         q_copies[r].start()
     key_spans(0)
 
@@ -249,63 +256,64 @@
         c_copies[1].start()
 
     key_spans(2)
-
-    @pl.when(c >= 4)
-    def _():
-        c_copies[4].wait_recv()
-
-    @pl.when(core == 1)
-    def _():
-        c_copies[3].start()
-
-    key_spans(4)
     c_copies[1].wait_recv()
     key_spans(1)
-    c_copies[3].wait_recv()
-    key_spans(3)
+
+    def receive_farther_blocks():
+        @pl.when(c >= 4)
+        def _():
+            c_copies[4].wait_recv()
+
+        @pl.when(core == 1)
+        def _():
+            c_copies[3].start()
+
+        key_spans(4)
+        c_copies[3].wait_recv()
+        key_spans(3)
 
     half = BLOCK // 2
 
-    def attend(p, first_keys, last_keys):
+    rows_of = [slice(0, half), slice(half, BLOCK)]
+
+    def score(p, d, k, g, top, buffer):
         extra = aug_q[pl.ds(pl.multiple_of(p * ROWS, ROWS), ROWS)]
         extra = jnp.concatenate([extra] * (GROUP // 2), axis=0)
-        spans = [(0, first_keys)] + [(0, BLOCK)] * 3 + [(last_keys, BLOCK)]
-
-        def queries_of(g):
-            heads = [qb[p, :, i * D:(i + 1) * D] for i in range(g * GROUP // 2, (g + 1) * GROUP // 2)]
-            return jnp.concatenate([jnp.concatenate(heads, axis=0), extra], axis=1)
-
-        def pieces(d):
-            start, stop = spans[d]
-            return [(k, g) for g in range(2) for k in range(start, stop, half)]
-
-        def score(d, k, g, top):
-            extra_keys = aug_k[d, k:k + half]
-            if d == 0:
-                column = iota((half, D), 1)
-                late = (iota((half, D), 0) + k - p * ROWS > column - (D - ROWS)) & (column >= D - ROWS)
-                extra_keys = jnp.where(late, BIG, extra_keys.astype(F32)).astype(BF16)
-            keys = jnp.concatenate([kvb[d, k:k + half], extra_keys], axis=1)
-            scores = nt_dot(keys, queries_of(g))
-            s_buf[d % 2, k:k + half, g * half:(g + 1) * half] = scores
-            here = jnp.max(scores.reshape(half // 8, 8, half), axis=0)
-            top[g] = here if top[g] is None else jnp.maximum(top[g], here)
-
-        def values_of(d, k):
-            parts = [kvb[d, BLOCK + part * D:BLOCK + (part + 1) * D] for part in range(k // D, (k + half) // D)]
-            return jnp.concatenate(parts, axis=1)
-
-        top = [None, None]
-        for k, g in pieces(0):
-            score(0, k, g, top)
-        running, total, accum = [None, None], [None, None], [None, None]
-        for d in range(STEPS + 1):
+        heads = [qb[p, :, n * D:(n + 1) * D] for n in range(g * GROUP // 2, (g + 1) * GROUP // 2)]
+        queries = jnp.concatenate([jnp.concatenate(heads, axis=0), extra], axis=1)
+        extra_keys = aug_k[d, k:k + half]
+        if d == 0:
+            column = iota((half, D), 1)
+            late = (iota((half, D), 0) + k - p * ROWS > column - (D - ROWS)) & (column >= D - ROWS)
+            extra_keys = jnp.where(late, BIG, extra_keys.astype(F32)).astype(BF16)
+        keys = jnp.concatenate([kvb[d, k:k + half], extra_keys], axis=1)
+        scores = nt_dot(keys, queries)
+        s_buf[buffer, k:k + half, rows_of[g]] = scores
+        here = jnp.max(scores.reshape(half // 8, 8, half), axis=0)
+        top[g] = here if top[g] is None else jnp.maximum(top[g], here)
+
+    def values_of(d, k):
+        parts = [kvb[d, BLOCK + part * D:BLOCK + (part + 1) * D] for part in range(k // D, (k + half) // D)]
+        return jnp.concatenate(parts, axis=1)
+
+    def pieces(span):
+        return [(k, g) for g in range(2) for k in range(*span, half)]
+
+    def attend(n, p, following, steps, spans, buffers):
+        top = [top_s[:, rows_of[g]] for g in range(2)]
+        if steps[0]:
+            running = [m_s[n, :, rows_of[g]] for g in range(2)]
+            total = [l_s[n, :, rows_of[g]] for g in range(2)]
+            accum = [o_s[n, :, rows_of[g]] for g in range(2)]
+        else:
+            running, total, accum = [None, None], [None, None], [None, None]
+        for place, d in enumerate(steps):
             next_top = [None, None]
-            now = pieces(d)
-            following = pieces(d + 1) if d < STEPS else []
-            for slot in range(max(len(now), len(following))):
-                if slot < len(following):
-                    score(d + 1, *following[slot], next_top)
+            later = (p, steps[place + 1]) if d != steps[-1] else (following, steps[0])
+            now, ahead = pieces(spans[d]), pieces(spans[later[1]])
+            for slot in range(max(len(now), len(ahead))):
+                if slot < len(ahead):
+                    score(*later, *ahead[slot], next_top, buffers[later[1]])
                 if slot >= len(now):
                     continue
                 k, g = now[slot]
@@ -318,49 +326,71 @@
                         accum[g] = accum[g] * factor
                     running[g] = newmax
                     top[g] = None
-                scores = s_buf[d % 2, k:k + half, g * half:(g + 1) * half]
+                scores = s_buf[buffers[d], k:k + half, rows_of[g]]
                 weights = jnp.exp2((scores - running[g]) * LOG2E_SCALE)
                 sums = jnp.sum(weights.reshape(half // 8, 8, half), axis=0)
                 product = jnp.dot(values_of(d, k), weights.astype(BF16), preferred_element_type=F32)
                 total[g] = sums if total[g] is None else total[g] + sums
                 accum[g] = product if accum[g] is None else accum[g] + product
             top = next_top
+        rows = pl.ds(pl.multiple_of(p * ROWS, ROWS), ROWS)
         for g in range(2):
+            top_s[:, rows_of[g]] = top[g]
+            if steps[-1] < STEPS:
+                m_s[n, :, rows_of[g]], l_s[n, :, rows_of[g]], o_s[n, :, rows_of[g]] = running[g], total[g], accum[g]
+                continue
             attended = accum[g] * (1.0 / jnp.sum(total[g], axis=0, keepdims=True))
             attended = attended.T.astype(BF16)
-            rows = pl.ds(pl.multiple_of(p * ROWS, ROWS), ROWS)
-            for i in range(GROUP // 2):
-                column = (g * GROUP // 2 + i) * D
-                out_ref[rows, column:column + D] = attended[i * ROWS:(i + 1) * ROWS]
-
-    def body(i, carry):
-        turn, rx = lax.rem(i, 4), i // 4
-        ry = turn + (turn // 2) * (5 - 2 * turn)
-        p = lax.rem(hy + 4 - ry, 4) * 2 + lax.rem(hx + rx, 2)
-
-        @pl.when(i == 0)
+            for member in range(GROUP // 2):
+                column = (g * GROUP // 2 + member) * D
+                out_ref[rows, column:column + D] = attended[member * ROWS:(member + 1) * ROWS]
+
+    def await_queries(turn, n):
+        p = partner(turn, n)
+        pltpu.make_async_remote_copy(
+            src_ref=q_columns(h), dst_ref=qb.at[p],
+            send_sem=q_send.at[0], recv_sem=q_recv.at[p],
+            device_id=(c, lax.rem(h + 1, PEERS)), device_id_type=MESH,
+        ).wait_recv()
+
+    def four_chunks(turn, steps, spans, buffers):
+        top = [None, None]
+        for k, g in pieces(spans[steps[0]]):
+            score(partner(turn, 0), steps[0], k, g, top, buffers[steps[0]])
+        for g in range(2):
+            top_s[:, rows_of[g]] = top[g]
+
+        def body(n, carry):
+            if not steps[0]:
+                @pl.when(n < 3)
+                def _():
+                    await_queries(turn, n + 1)
+
+            attend(n, partner(turn, n), partner(turn, jnp.minimum(n + 1, 3)), steps, spans, buffers)
+            return carry
+
+        lax.fori_loop(0, 4, body, 0)
+
+    whole = (0, BLOCK)
+    early = {0: (0, half), 1: whole, 2: whole, 3: whole, 4: whole}
+    late = {0: whole, 1: whole, 2: whole, 3: whole, 4: (half, BLOCK)}
+    own_early = hy < 2
+
+    def either(first, *arguments):
+        @pl.when(first)
         def _():
-            own_q.wait()
-
-        @pl.when(i > 0)
+            four_chunks(*arguments[:2], early, arguments[2])
+
+        @pl.when(jnp.logical_not(first))
         def _():
-            pltpu.make_async_remote_copy(
-                src_ref=q_columns(h), dst_ref=qb.at[p],
-                send_sem=q_send.at[0], recv_sem=q_recv.at[p],
-                device_id=(c, lax.rem(h + 1, PEERS)), device_id_type=MESH,
-            ).wait_recv()
-
-        @pl.when(p < PEERS // 2)
-        def _():
-            attend(p, half, 0)
-
-        @pl.when(p >= PEERS // 2)
-        def _():
-            attend(p, BLOCK, half)
-
-        return carry
-
-    lax.fori_loop(0, PEERS, body, 0)
+            four_chunks(*arguments[:2], late, arguments[2])
+
+    own_q.wait()
+    either(own_early, 0, (0, 1, 2), {0: 0, 1: 1, 2: 2})
+    receive_farther_blocks()
+    either(own_early, 0, (3, 4), {3: 0, 4: 1})
+    await_queries(1, 0)
+    either(jnp.logical_not(own_early), 1, (0, 1, 2, 3, 4), {0: 0, 1: 1, 2: 0, 3: 1, 4: 2})
 
     for r in range(1, PEERS):
         kv_copies[r].wait_send()
@@ -400,7 +430,11 @@
             pltpu.VMEM((PEERS, ROWS, GROUP * D), BF16),
             pltpu.VMEM((BLOCK, D), BF16),
             pltpu.VMEM((STEPS + 1, BLOCK, D), BF16),
-            pltpu.VMEM((2, BLOCK, BLOCK), F32),
+            pltpu.VMEM((3, BLOCK, BLOCK), F32),
+            pltpu.VMEM((8, BLOCK), F32),
+            pltpu.VMEM((4, 1, BLOCK), F32),
+            pltpu.VMEM((4, 8, BLOCK), F32),
+            pltpu.VMEM((4, D, BLOCK), F32),
             dma((7,)), dma((PEERS,)), dma((PEERS,)), dma((PEERS,)), dma((PEERS,)),
             dma((PEERS + 1,)), dma((PEERS + 1,)), dma((STEPS + 1,)), dma((STEPS + 1,)),
         ],

time: 39.8 us -> 39.4 us (0.990)
  the two profiles are of different devices: /device:TPU:224 before, /device:TPU:100 now
where the time goes in v2:
time: 39.4 us; the launch traced here: 39.1 us
  Pallas kernels  36.8 us (93%)
  local copies, waits for them, and re-layouts  2.26 us (6%)
    pallas_call x1, Pallas kernels, per_device(): pl.pallas_call(kernel, out_shape=jax.ShapeDtypeStruct((BLOCK, GROUP * D),...  36.8 us
    unnamed x1, local copies, waits for them, and re-layouts  2.26 us

profile of v2, /device:TPU:100, one launch (start us, length us, event | category | flops | bytes accessed | tf_op | source)
XLA Modules:
  0.0 39.1 jit_solution(12646622444966210841)
XLA Ops:
  0.0 36.8 %shard_map.64 = bf16[512,1024]{1,0:T(8,128)(2,1)} custom-call(bf16[64,8192]{1,0:T(8,128)(2,1)} %q_hbm.1, bf16[64,1024]{1,0:T(8,128)(2,1)} %kc_hbm.1, bf16[64,1024]{1,0:T(8,128)(2,1)} %vc_hbm.1, s32[8,64]{1,0:T(8,128)} %bitcast.3, s32[8,64]{1,0:T(8,128)} %bitcast.4, s32[1,512]{1,0:T(1,128)} %bitcast.5), custom_call_target="tpu_custom_call" | custom-call | flops 8999999488 | bytes 4000000 | tf_op jit(solution)/shard_map/pallas_call | solution.py:414
  36.8 2.3 %copy.8 = bf16[512,1024]{1,0:T(8,128)(2,1)} copy(bf16[512,1024]{1,0:T(8,128)(2,1)} %shard_map.64) | data formatting | bytes 2097152

commit v3 on v2

--- a/solution.py
+++ b/solution.py
@@ -35,7 +35,7 @@
 def kernel(
     q_hbm, kc_hbm, vc_hbm, ke_hbm, ve_hbm, ids_hbm, out_ref,
     q_ref, kc_ref, vc_ref, ke_ref, ve_ref, ids_ref,
-    kvs, kvr, kvr2, kvb, qb, aug_q, aug_k, s_buf, top_s, m_s, l_s, o_s,
+    kvs, kvr, kvr2, kvb, qb, qt, aug_q, aug_k, s_buf, top_s, m_s, l_s, o_s,
     in_sem, kv_send, kv_recv, q_send, q_recv, a_send, a_recv, c_send, c_recv,
 ):
     c = lax.axis_index("ctx")
@@ -175,7 +175,7 @@
     q_copies = {r: q_copy(r) for r in range(1, PEERS)}
     fetches[5].wait()
     own_q.start()
-    for r in (1, 4, 5):
+    for r in (1, 2, 3, 4, 5):
         q_copies[r].start()
     kvr[my_rows] = kvs[h]
 
@@ -224,7 +224,7 @@
     def _():
         c_copies[1].start()
 
-    for r in (2, 3, 6, 7):
+    for r in (6, 7):
         q_copies[r].start()
     key_spans(0)
 
@@ -259,14 +259,17 @@
     c_copies[1].wait_recv()
     key_spans(1)
 
-    def receive_farther_blocks():
+    def pass_on_farther_block():
         @pl.when(c >= 4)
         def _():
             c_copies[4].wait_recv()
 
-        @pl.when(core == 1)
+        c_copies[3].start()
+
+    def receive_farther_blocks():
+        @pl.when((core == 0) & (c >= 4))
         def _():
-            c_copies[3].start()
+            c_copies[4].wait_recv()
 
         key_spans(4)
         c_copies[3].wait_recv()
@@ -276,18 +279,22 @@
 
     rows_of = [slice(0, half), slice(half, BLOCK)]
 
-    def score(p, d, k, g, top, buffer):
+    def turn_queries(n, p):
+        for g in range(2):
+            heads = [qb[p, :, m * D:(m + 1) * D] for m in range(g * GROUP // 2, (g + 1) * GROUP // 2)]
+            qt[n, g] = jnp.concatenate(heads, axis=0).T
         extra = aug_q[pl.ds(pl.multiple_of(p * ROWS, ROWS), ROWS)]
-        extra = jnp.concatenate([extra] * (GROUP // 2), axis=0)
-        heads = [qb[p, :, n * D:(n + 1) * D] for n in range(g * GROUP // 2, (g + 1) * GROUP // 2)]
-        queries = jnp.concatenate([jnp.concatenate(heads, axis=0), extra], axis=1)
+        qt[n, 2] = jnp.concatenate([extra] * (GROUP // 2), axis=0).T
+
+    def score(n, p, d, k, g, top, buffer):
+        queries = jnp.concatenate([qt[n, g], qt[n, 2]], axis=0)
         extra_keys = aug_k[d, k:k + half]
         if d == 0:
             column = iota((half, D), 1)
             late = (iota((half, D), 0) + k - p * ROWS > column - (D - ROWS)) & (column >= D - ROWS)
             extra_keys = jnp.where(late, BIG, extra_keys.astype(F32)).astype(BF16)
         keys = jnp.concatenate([kvb[d, k:k + half], extra_keys], axis=1)
-        scores = nt_dot(keys, queries)
+        scores = jnp.dot(keys, queries, preferred_element_type=F32)
         s_buf[buffer, k:k + half, rows_of[g]] = scores
         here = jnp.max(scores.reshape(half // 8, 8, half), axis=0)
         top[g] = here if top[g] is None else jnp.maximum(top[g], here)
@@ -309,11 +316,11 @@
             running, total, accum = [None, None], [None, None], [None, None]
         for place, d in enumerate(steps):
             next_top = [None, None]
-            later = (p, steps[place + 1]) if d != steps[-1] else (following, steps[0])
-            now, ahead = pieces(spans[d]), pieces(spans[later[1]])
+            later = (n, p, steps[place + 1]) if d != steps[-1] else (*following, steps[0])
+            now, ahead = pieces(spans[d]), pieces(spans[later[2]])
             for slot in range(max(len(now), len(ahead))):
                 if slot < len(ahead):
-                    score(*later, *ahead[slot], next_top, buffers[later[1]])
+                    score(*later, *ahead[slot], next_top, buffers[later[2]])
                 if slot >= len(now):
                     continue
                 k, g = now[slot]
@@ -354,19 +361,28 @@
         ).wait_recv()
 
     def four_chunks(turn, steps, spans, buffers):
+        if not steps[0]:
+            turn_queries(0, partner(turn, 0))
         top = [None, None]
         for k, g in pieces(spans[steps[0]]):
-            score(partner(turn, 0), steps[0], k, g, top, buffers[steps[0]])
+            score(0, partner(turn, 0), steps[0], k, g, top, buffers[steps[0]])
         for g in range(2):
             top_s[:, rows_of[g]] = top[g]
 
         def body(n, carry):
+            if steps == (0, 1, 2):
+                @pl.when((n == 2) & (core == 1))
+                def _():
+                    pass_on_farther_block()
+
             if not steps[0]:
                 @pl.when(n < 3)
                 def _():
                     await_queries(turn, n + 1)
-
-            attend(n, partner(turn, n), partner(turn, jnp.minimum(n + 1, 3)), steps, spans, buffers)
+                    turn_queries(n + 1, partner(turn, n + 1))
+
+            after = jnp.minimum(n + 1, 3)
+            attend(n, partner(turn, n), (after, partner(turn, after)), steps, spans, buffers)
             return carry
 
         lax.fori_loop(0, 4, body, 0)
@@ -428,6 +444,7 @@
             pltpu.VMEM((BLOCK, 2 * D), BF16),
             pltpu.VMEM((STEPS + 1, KV_ROWS, D), BF16),
             pltpu.VMEM((PEERS, ROWS, GROUP * D), BF16),
+            pltpu.VMEM((4, 3, D, BLOCK // 2), BF16),
             pltpu.VMEM((BLOCK, D), BF16),
             pltpu.VMEM((STEPS + 1, BLOCK, D), BF16),
             pltpu.VMEM((3, BLOCK, BLOCK), F32),

time: 39.4 us -> 38.8 us (0.985)
  the two profiles are of different devices: /device:TPU:100 before, /device:TPU:6 now
where the time goes in v3:
time: 38.8 us; the launch traced here: 38.7 us
  Pallas kernels  36.4 us (94%)
  local copies, waits for them, and re-layouts  2.26 us (6%)
    pallas_call x1, Pallas kernels, per_device(): pl.pallas_call(kernel, out_shape=jax.ShapeDtypeStruct((BLOCK, GROUP * D),...  36.4 us
    unnamed x1, local copies, waits for them, and re-layouts  2.26 us

profile of v3, /device:TPU:6, one launch (start us, length us, event | category | flops | bytes accessed | tf_op | source)
XLA Modules:
  0.0 38.7 jit_solution(6693724719451453258)
XLA Ops:
  0.0 36.4 %shard_map.64 = bf16[512,1024]{1,0:T(8,128)(2,1)} custom-call(bf16[64,8192]{1,0:T(8,128)(2,1)} %q_hbm.1, bf16[64,1024]{1,0:T(8,128)(2,1)} %kc_hbm.1, bf16[64,1024]{1,0:T(8,128)(2,1)} %vc_hbm.1, s32[8,64]{1,0:T(8,128)} %bitcast.3, s32[8,64]{1,0:T(8,128)} %bitcast.4, s32[1,512]{1,0:T(1,128)} %bitcast.5), custom_call_target="tpu_custom_call" | custom-call | flops 8999999488 | bytes 4000000 | tf_op jit(solution)/shard_map/pallas_call | solution.py:430
  36.4 2.3 %copy.8 = bf16[512,1024]{1,0:T(8,128)(2,1)} copy(bf16[512,1024]{1,0:T(8,128)(2,1)} %shard_map.64) | data formatting | bytes 2097152

commit v4 on v3

--- a/solution.py
+++ b/solution.py
@@ -33,10 +33,10 @@
 
 
 def kernel(
-    q_hbm, kc_hbm, vc_hbm, ke_hbm, ve_hbm, ids_hbm, out_ref,
+    q_hbm, kc_hbm, vc_hbm, ke_hbm, ve_hbm, ids_hbm, out_hbm,
     q_ref, kc_ref, vc_ref, ke_ref, ve_ref, ids_ref,
-    kvs, kvr, kvr2, kvb, qb, qt, aug_q, aug_k, s_buf, top_s, m_s, l_s, o_s,
-    in_sem, kv_send, kv_recv, q_send, q_recv, a_send, a_recv, c_send, c_recv,
+    kvs, kvr, kvr2, kvb, qb, qt, aug_q, aug_k, s_buf, top_s, m_s, l_s, o_s, ob,
+    in_sem, kv_send, kv_recv, q_send, q_recv, a_send, a_recv, c_send, c_recv, out_sem,
 ):
     c = lax.axis_index("ctx")
     h = lax.axis_index("head")
@@ -277,80 +277,67 @@
 
     half = BLOCK // 2
 
-    rows_of = [slice(0, half), slice(half, BLOCK)]
-
     def turn_queries(n, p):
-        for g in range(2):
-            heads = [qb[p, :, m * D:(m + 1) * D] for m in range(g * GROUP // 2, (g + 1) * GROUP // 2)]
-            qt[n, g] = jnp.concatenate(heads, axis=0).T
+        qt[n, 0:D] = jnp.concatenate([qb[p, :, m * D:(m + 1) * D] for m in range(GROUP)], axis=0).T
         extra = aug_q[pl.ds(pl.multiple_of(p * ROWS, ROWS), ROWS)]
-        qt[n, 2] = jnp.concatenate([extra] * (GROUP // 2), axis=0).T
-
-    def score(n, p, d, k, g, top, buffer):
-        queries = jnp.concatenate([qt[n, g], qt[n, 2]], axis=0)
+        extra = jnp.concatenate([extra] * 2, axis=0).T
+        qt[n, D:2 * D] = jnp.concatenate([extra] * (GROUP // 2), axis=1)
+
+    def score(n, p, d, k, top, buffer):
         extra_keys = aug_k[d, k:k + half]
         if d == 0:
             column = iota((half, D), 1)
             late = (iota((half, D), 0) + k - p * ROWS > column - (D - ROWS)) & (column >= D - ROWS)
             extra_keys = jnp.where(late, BIG, extra_keys.astype(F32)).astype(BF16)
         keys = jnp.concatenate([kvb[d, k:k + half], extra_keys], axis=1)
-        scores = jnp.dot(keys, queries, preferred_element_type=F32)
-        s_buf[buffer, k:k + half, rows_of[g]] = scores
-        here = jnp.max(scores.reshape(half // 8, 8, half), axis=0)
-        top[g] = here if top[g] is None else jnp.maximum(top[g], here)
+        scores = jnp.dot(keys, qt[n], preferred_element_type=F32)
+        s_buf[buffer, k:k + half] = scores
+        here = jnp.max(scores.reshape(half // 8, 8, BLOCK), axis=0)
+        return here if top is None else jnp.maximum(top, here)
 
     def values_of(d, k):
         parts = [kvb[d, BLOCK + part * D:BLOCK + (part + 1) * D] for part in range(k // D, (k + half) // D)]
         return jnp.concatenate(parts, axis=1)
 
-    def pieces(span):
-        return [(k, g) for g in range(2) for k in range(*span, half)]
+    def out_copy(p):
+        rows = pl.ds(pl.multiple_of(p * ROWS, ROWS), ROWS)
+        return pltpu.make_async_copy(ob.at[p], out_hbm.at[rows], out_sem.at[p])
 
     def attend(n, p, following, steps, spans, buffers):
-        top = [top_s[:, rows_of[g]] for g in range(2)]
-        if steps[0]:
-            running = [m_s[n, :, rows_of[g]] for g in range(2)]
-            total = [l_s[n, :, rows_of[g]] for g in range(2)]
-            accum = [o_s[n, :, rows_of[g]] for g in range(2)]
-        else:
-            running, total, accum = [None, None], [None, None], [None, None]
+        top = top_s[...]
+        running, total, accum = (m_s[n], l_s[n], o_s[n]) if steps[0] else (None, None, None)
         for place, d in enumerate(steps):
-            next_top = [None, None]
+            next_top = None
             later = (n, p, steps[place + 1]) if d != steps[-1] else (*following, steps[0])
-            now, ahead = pieces(spans[d]), pieces(spans[later[2]])
+            now, ahead = list(range(*spans[d], half)), list(range(*spans[later[2]], half))
+            newmax = jnp.max(top, axis=0, keepdims=True)
+            if d:
+                newmax = jnp.maximum(running, newmax)
+                factor = jnp.exp2((running - newmax) * LOG2E_SCALE)
+                total = total * factor
+                accum = accum * factor
+            running = newmax
             for slot in range(max(len(now), len(ahead))):
                 if slot < len(ahead):
-                    score(*later, *ahead[slot], next_top, buffers[later[2]])
+                    next_top = score(*later, ahead[slot], next_top, buffers[later[2]])
                 if slot >= len(now):
                     continue
-                k, g = now[slot]
-                if top[g] is not None:
-                    newmax = jnp.max(top[g], axis=0, keepdims=True)
-                    if d:
-                        newmax = jnp.maximum(running[g], newmax)
-                        factor = jnp.exp2((running[g] - newmax) * LOG2E_SCALE)
-                        total[g] = total[g] * factor
-                        accum[g] = accum[g] * factor
-                    running[g] = newmax
-                    top[g] = None
-                scores = s_buf[buffers[d], k:k + half, rows_of[g]]
-                weights = jnp.exp2((scores - running[g]) * LOG2E_SCALE)
-                sums = jnp.sum(weights.reshape(half // 8, 8, half), axis=0)
+                k = now[slot]
+                weights = jnp.exp2((s_buf[buffers[d], k:k + half] - running) * LOG2E_SCALE)
+                sums = jnp.sum(weights.reshape(half // 8, 8, BLOCK), axis=0)
                 product = jnp.dot(values_of(d, k), weights.astype(BF16), preferred_element_type=F32)
-                total[g] = sums if total[g] is None else total[g] + sums
-                accum[g] = product if accum[g] is None else accum[g] + product
+                total = sums if total is None else total + sums
+                accum = product if accum is None else accum + product
             top = next_top
-        rows = pl.ds(pl.multiple_of(p * ROWS, ROWS), ROWS)
-        for g in range(2):
-            top_s[:, rows_of[g]] = top[g]
-            if steps[-1] < STEPS:
-                m_s[n, :, rows_of[g]], l_s[n, :, rows_of[g]], o_s[n, :, rows_of[g]] = running[g], total[g], accum[g]
-                continue
-            attended = accum[g] * (1.0 / jnp.sum(total[g], axis=0, keepdims=True))
-            attended = attended.T.astype(BF16)
-            for member in range(GROUP // 2):
-                column = (g * GROUP // 2 + member) * D
-                out_ref[rows, column:column + D] = attended[member * ROWS:(member + 1) * ROWS]
+        top_s[...] = top
+        if steps[-1] < STEPS:
+            m_s[n], l_s[n], o_s[n] = running, total, accum
+            return
+        attended = accum * (1.0 / jnp.sum(total, axis=0, keepdims=True))
+        attended = attended.T.astype(BF16)
+        for member in range(GROUP):
+            ob[p, :, member * D:(member + 1) * D] = attended[member * ROWS:(member + 1) * ROWS]
+        out_copy(p).start()
 
     def await_queries(turn, n):
         p = partner(turn, n)
@@ -363,11 +350,10 @@
     def four_chunks(turn, steps, spans, buffers):
         if not steps[0]:
             turn_queries(0, partner(turn, 0))
-        top = [None, None]
-        for k, g in pieces(spans[steps[0]]):
-            score(0, partner(turn, 0), steps[0], k, g, top, buffers[steps[0]])
-        for g in range(2):
-            top_s[:, rows_of[g]] = top[g]
+        top = None
+        for k in range(*spans[steps[0]], half):
+            top = score(0, partner(turn, 0), steps[0], k, top, buffers[steps[0]])
+        top_s[...] = top
 
         def body(n, carry):
             if steps == (0, 1, 2):
@@ -408,6 +394,8 @@
     await_queries(1, 0)
     either(jnp.logical_not(own_early), 1, (0, 1, 2, 3, 4), {0: 0, 1: 1, 2: 0, 3: 1, 4: 2})
 
+    for p in range(PEERS):
+        out_copy(p).wait()
     for r in range(1, PEERS):
         kv_copies[r].wait_send()
         q_copies[r].wait_send()
@@ -431,7 +419,7 @@
         kernel,
         out_shape=jax.ShapeDtypeStruct((BLOCK, GROUP * D), BF16),
         in_specs=[hbm] * 6,
-        out_specs=pl.BlockSpec(memory_space=pltpu.VMEM),
+        out_specs=hbm,
         scratch_shapes=[
             pltpu.VMEM((ROWS, PEERS * GROUP * D), BF16),
             pltpu.VMEM((ROWS, PEERS * D), BF16),
@@ -444,7 +432,7 @@
             pltpu.VMEM((BLOCK, 2 * D), BF16),
             pltpu.VMEM((STEPS + 1, KV_ROWS, D), BF16),
             pltpu.VMEM((PEERS, ROWS, GROUP * D), BF16),
-            pltpu.VMEM((4, 3, D, BLOCK // 2), BF16),
+            pltpu.VMEM((4, 2 * D, BLOCK), BF16),
             pltpu.VMEM((BLOCK, D), BF16),
             pltpu.VMEM((STEPS + 1, BLOCK, D), BF16),
             pltpu.VMEM((3, BLOCK, BLOCK), F32),
@@ -452,8 +440,9 @@
             pltpu.VMEM((4, 1, BLOCK), F32),
             pltpu.VMEM((4, 8, BLOCK), F32),
             pltpu.VMEM((4, D, BLOCK), F32),
+            pltpu.VMEM((PEERS, ROWS, GROUP * D), BF16),
             dma((7,)), dma((PEERS,)), dma((PEERS,)), dma((PEERS,)), dma((PEERS,)),
-            dma((PEERS + 1,)), dma((PEERS + 1,)), dma((STEPS + 1,)), dma((STEPS + 1,)),
+            dma((PEERS + 1,)), dma((PEERS + 1,)), dma((STEPS + 1,)), dma((STEPS + 1,)), dma((PEERS,)),
         ],
         compiler_params=pltpu.CompilerParams(
             collective_id=0, has_side_effects=True, vmem_limit_bytes=62 * 1024 * 1024

time: 38.8 us -> 40.7 us (1.049)
  Pallas kernels: 36.4 us -> 38.3 us
    pallas_call x1, Pallas kernels: 36.4 us -> 38.3 us  [per_device(): pl.pallas_call(kernel, out_shape=jax.ShapeDtypeStruct((BLOCK, GROUP * D),...]
where the time goes in v4:
time: 40.7 us; the launch traced here: 40.6 us
  Pallas kernels  38.3 us (94%)
  local copies, waits for them, and re-layouts  2.26 us (6%)
    pallas_call x1, Pallas kernels, per_device(): pl.pallas_call(kernel, out_shape=jax.ShapeDtypeStruct((BLOCK, GROUP * D),...  38.3 us
    unnamed x1, local copies, waits for them, and re-layouts  2.26 us

profile of v4, /device:TPU:6, one launch (start us, length us, event | category | flops | bytes accessed | tf_op | source)
XLA Modules:
  0.0 40.6 jit_solution(15004033988848735489)
XLA Ops:
  0.0 38.3 %shard_map.64 = bf16[512,1024]{1,0:T(8,128)(2,1)} custom-call(bf16[64,8192]{1,0:T(8,128)(2,1)} %q_hbm.1, bf16[64,1024]{1,0:T(8,128)(2,1)} %kc_hbm.1, bf16[64,1024]{1,0:T(8,128)(2,1)} %vc_hbm.1, s32[8,64]{1,0:T(8,128)} %bitcast.3, s32[8,64]{1,0:T(8,128)} %bitcast.4, s32[1,512]{1,0:T(1,128)} %bitcast.5), custom_call_target="tpu_custom_call" | custom-call | flops 8999999488 | bytes 4000000 | tf_op jit(solution)/shard_map/pallas_call | solution.py:418
  38.3 2.3 %copy.8 = bf16[512,1024]{1,0:T(8,128)(2,1)} copy(bf16[512,1024]{1,0:T(8,128)(2,1)} %shard_map.64) | data formatting | bytes 2097152

commit v5 on v3

--- a/solution.py
+++ b/solution.py
@@ -33,10 +33,10 @@
 
 
 def kernel(
-    q_hbm, kc_hbm, vc_hbm, ke_hbm, ve_hbm, ids_hbm, out_ref,
+    q_hbm, kc_hbm, vc_hbm, ke_hbm, ve_hbm, ids_hbm, out_hbm,
     q_ref, kc_ref, vc_ref, ke_ref, ve_ref, ids_ref,
-    kvs, kvr, kvr2, kvb, qb, qt, aug_q, aug_k, s_buf, top_s, m_s, l_s, o_s,
-    in_sem, kv_send, kv_recv, q_send, q_recv, a_send, a_recv, c_send, c_recv,
+    kvs, kvr, kvr2, kvb, qb, qt, aug_q, aug_k, s_buf, top_s, m_s, l_s, o_s, ob,
+    in_sem, kv_send, kv_recv, q_send, q_recv, a_send, a_recv, c_send, c_recv, out_sem,
 ):
     c = lax.axis_index("ctx")
     h = lax.axis_index("head")
@@ -228,36 +228,35 @@
         q_copies[r].start()
     key_spans(0)
 
-    @pl.when(c >= 2)
-    def _():
-        for j in range(PEERS):
-            pltpu.make_async_remote_copy(
-                src_ref=kvs.at[0], dst_ref=kvr2.at[j * ROWS:(j + 1) * ROWS],
-                send_sem=a_send.at[0], recv_sem=a_recv.at[j],
-                device_id=(after2, h), device_id_type=MESH,
-            ).wait_recv()
-        a_copies[PEERS].wait_recv()
-        rotate(kvr2, 2)
-
-    @pl.when(c < 2)
-    def _():
-        kvb[2] = jnp.zeros((KV_ROWS, D), BF16)
-
-    @pl.when(c < 4)
-    def _():
-        kvb[4] = jnp.zeros((KV_ROWS, D), BF16)
-
-    @pl.when(core == 0)
-    def _():
-        c_copies[3].start()
-
-    @pl.when(core == 1)
-    def _():
-        c_copies[1].start()
-
-    key_spans(2)
-    c_copies[1].wait_recv()
-    key_spans(1)
+    def receive_nearer_blocks():
+        @pl.when(c >= 2)
+        def _():
+            for j in range(PEERS):
+                pltpu.make_async_remote_copy(
+                    src_ref=kvs.at[0], dst_ref=kvr2.at[j * ROWS:(j + 1) * ROWS],
+                    send_sem=a_send.at[0], recv_sem=a_recv.at[j],
+                    device_id=(after2, h), device_id_type=MESH,
+                ).wait_recv()
+            a_copies[PEERS].wait_recv()
+            rotate(kvr2, 2)
+
+        @pl.when(c < 2)
+        def _():
+            kvb[2] = jnp.zeros((KV_ROWS, D), BF16)
+
+        @pl.when(c < 4)
+        def _():
+            kvb[4] = jnp.zeros((KV_ROWS, D), BF16)
+
+        @pl.when(core == 0)
+        def _():
+            c_copies[3].start()
+
+        @pl.when(core == 1)
+        def _():
+            c_copies[1].start()
+
+        key_spans(2)
 
     def pass_on_farther_block():
         @pl.when(c >= 4)
@@ -303,8 +302,22 @@
         parts = [kvb[d, BLOCK + part * D:BLOCK + (part + 1) * D] for part in range(k // D, (k + half) // D)]
         return jnp.concatenate(parts, axis=1)
 
+    def out_copy(p):
+        rows = pl.ds(pl.multiple_of(p * ROWS, ROWS), ROWS)
+        return pltpu.make_async_copy(ob.at[p], out_hbm.at[rows], out_sem.at[p])
+
     def pieces(span):
         return [(k, g) for g in range(2) for k in range(*span, half)]
+
+    def weigh(d, k, g, buffer, newmax):
+        sums, low = None, []
+        for row in range(k, k + half, ROWS):
+            weights = jnp.exp2((s_buf[buffer, row:row + ROWS, rows_of[g]] - newmax) * LOG2E_SCALE)
+            added = jnp.sum(weights.reshape(ROWS // 8, 8, half), axis=0)
+            sums = added if sums is None else sums + added
+            low.append(weights.astype(BF16))
+        low = jnp.concatenate(low, axis=0)
+        return sums, jnp.dot(values_of(d, k), low, preferred_element_type=F32)
 
     def attend(n, p, following, steps, spans, buffers):
         top = [top_s[:, rows_of[g]] for g in range(2)]
@@ -333,14 +346,10 @@
                         accum[g] = accum[g] * factor
                     running[g] = newmax
                     top[g] = None
-                scores = s_buf[buffers[d], k:k + half, rows_of[g]]
-                weights = jnp.exp2((scores - running[g]) * LOG2E_SCALE)
-                sums = jnp.sum(weights.reshape(half // 8, 8, half), axis=0)
-                product = jnp.dot(values_of(d, k), weights.astype(BF16), preferred_element_type=F32)
+                sums, product = weigh(d, k, g, buffers[d], running[g])
                 total[g] = sums if total[g] is None else total[g] + sums
                 accum[g] = product if accum[g] is None else accum[g] + product
             top = next_top
-        rows = pl.ds(pl.multiple_of(p * ROWS, ROWS), ROWS)
         for g in range(2):
             top_s[:, rows_of[g]] = top[g]
             if steps[-1] < STEPS:
@@ -350,7 +359,9 @@
             attended = attended.T.astype(BF16)
             for member in range(GROUP // 2):
                 column = (g * GROUP // 2 + member) * D
-                out_ref[rows, column:column + D] = attended[member * ROWS:(member + 1) * ROWS]
+                ob[p, :, column:column + D] = attended[member * ROWS:(member + 1) * ROWS]
+        if steps[-1] == STEPS:
+            out_copy(p).start()
 
     def await_queries(turn, n):
         p = partner(turn, n)
@@ -370,7 +381,7 @@
             top_s[:, rows_of[g]] = top[g]
 
         def body(n, carry):
-            if steps == (0, 1, 2):
+            if steps == (1, 2):
                 @pl.when((n == 2) & (core == 1))
                 def _():
                     pass_on_farther_block()
@@ -387,6 +398,33 @@
 
         lax.fori_loop(0, 4, body, 0)
 
+    def own_block(chunks, span):
+        tops = {}
+        for n in chunks:
+            p = partner(0, n)
+            if n:
+                await_queries(0, n)
+            turn_queries(n, p)
+            tops[n] = [None, None]
+            for k, g in pieces(span):
+                score(n, p, 0, k, g, tops[n], n % 2)
+        for n in chunks:
+            for g in range(2):
+                newmax = jnp.max(tops[n][g], axis=0, keepdims=True)
+                parts = [weigh(0, k, g, n % 2, newmax) for k in range(*span, half)]
+                m_s[n, :, rows_of[g]] = newmax
+                l_s[n, :, rows_of[g]] = sum([part[0] for part in parts[1:]], parts[0][0])
+                o_s[n, :, rows_of[g]] = sum([part[1] for part in parts[1:]], parts[0][1])
+
+    def either_own_block(chunks):
+        @pl.when(own_early)
+        def _():
+            own_block(chunks, early[0])
+
+        @pl.when(jnp.logical_not(own_early))
+        def _():
+            own_block(chunks, late[0])
+
     whole = (0, BLOCK)
     early = {0: (0, half), 1: whole, 2: whole, 3: whole, 4: whole}
     late = {0: whole, 1: whole, 2: whole, 3: whole, 4: (half, BLOCK)}
@@ -402,12 +440,19 @@
             four_chunks(*arguments[:2], late, arguments[2])
 
     own_q.wait()
-    either(own_early, 0, (0, 1, 2), {0: 0, 1: 1, 2: 2})
+    either_own_block((0, 1))
+    receive_nearer_blocks()
+    either_own_block((2, 3))
+    c_copies[1].wait_recv()
+    key_spans(1)
+    either(own_early, 0, (1, 2), {1: 0, 2: 1})
     receive_farther_blocks()
     either(own_early, 0, (3, 4), {3: 0, 4: 1})
     await_queries(1, 0)
     either(jnp.logical_not(own_early), 1, (0, 1, 2, 3, 4), {0: 0, 1: 1, 2: 0, 3: 1, 4: 2})
 
+    for p in range(PEERS):
+        out_copy(p).wait()
     for r in range(1, PEERS):
         kv_copies[r].wait_send()
         q_copies[r].wait_send()
@@ -431,7 +476,7 @@
         kernel,
         out_shape=jax.ShapeDtypeStruct((BLOCK, GROUP * D), BF16),
         in_specs=[hbm] * 6,
-        out_specs=pl.BlockSpec(memory_space=pltpu.VMEM),
+        out_specs=hbm,
         scratch_shapes=[
             pltpu.VMEM((ROWS, PEERS * GROUP * D), BF16),
             pltpu.VMEM((ROWS, PEERS * D), BF16),
@@ -452,8 +497,9 @@
             pltpu.VMEM((4, 1, BLOCK), F32),
             pltpu.VMEM((4, 8, BLOCK), F32),
             pltpu.VMEM((4, D, BLOCK), F32),
+            pltpu.VMEM((PEERS, ROWS, GROUP * D), BF16),
             dma((7,)), dma((PEERS,)), dma((PEERS,)), dma((PEERS,)), dma((PEERS,)),
-            dma((PEERS + 1,)), dma((PEERS + 1,)), dma((STEPS + 1,)), dma((STEPS + 1,)),
+            dma((PEERS + 1,)), dma((PEERS + 1,)), dma((STEPS + 1,)), dma((STEPS + 1,)), dma((PEERS,)),
         ],
         compiler_params=pltpu.CompilerParams(
             collective_id=0, has_side_effects=True, vmem_limit_bytes=62 * 1024 * 1024

time: 38.8 us -> 39.4 us (1.015)
  Pallas kernels: 36.4 us -> 37 us
    pallas_call x1, Pallas kernels: 36.4 us -> 37 us  [per_device(): pl.pallas_call(kernel, out_shape=jax.ShapeDtypeStruct((BLOCK, GROUP * D),...]
where the time goes in v5:
time: 39.4 us; the launch traced here: 39.3 us
  Pallas kernels  37 us (94%)
  local copies, waits for them, and re-layouts  2.26 us (6%)
    pallas_call x1, Pallas kernels, per_device(): pl.pallas_call(kernel, out_shape=jax.ShapeDtypeStruct((BLOCK, GROUP * D),...  37 us
    unnamed x1, local copies, waits for them, and re-layouts  2.26 us

profile of v5, /device:TPU:6, one launch (start us, length us, event | category | flops | bytes accessed | tf_op | source)
XLA Modules:
  0.0 39.3 jit_solution(172654327739171527)
XLA Ops:
  0.0 37.0 %shard_map.64 = bf16[512,1024]{1,0:T(8,128)(2,1)} custom-call(bf16[64,8192]{1,0:T(8,128)(2,1)} %q_hbm.1, bf16[64,1024]{1,0:T(8,128)(2,1)} %kc_hbm.1, bf16[64,1024]{1,0:T(8,128)(2,1)} %vc_hbm.1, s32[8,64]{1,0:T(8,128)} %bitcast.3, s32[8,64]{1,0:T(8,128)} %bitcast.4, s32[1,512]{1,0:T(1,128)} %bitcast.5), custom_call_target="tpu_custom_call" | custom-call | flops 8999999488 | bytes 4000000 | tf_op jit(solution)/shard_map/pallas_call | solution.py:475
  37.0 2.3 %copy.8 = bf16[512,1024]{1,0:T(8,128)(2,1)} copy(bf16[512,1024]{1,0:T(8,128)(2,1)} %shard_map.64) | data formatting | bytes 2097152

commit v6 on v1

--- a/solution.py
+++ b/solution.py
@@ -33,10 +33,10 @@
 
 
 def kernel(
-    q_hbm, kc_hbm, vc_hbm, ke_hbm, ve_hbm, ids_hbm, out_ref,
+    q_hbm, kc_hbm, vc_hbm, ke_hbm, ve_hbm, ids_hbm, out_hbm,
     q_ref, kc_ref, vc_ref, ke_ref, ve_ref, ids_ref,
-    kvs, kvr, kvr2, kvb, qb, aug_q, aug_k, s_buf,
-    in_sem, kv_send, kv_recv, q_send, q_recv, a_send, a_recv, c_send, c_recv,
+    kvs, kvr, kvr2, kvb, qb, aug_q, aug_k, s_buf, ob,
+    in_sem, kv_send, kv_recv, q_send, q_recv, a_send, a_recv, c_send, c_recv, out_sem,
 ):
     c = lax.axis_index("ctx")
     h = lax.axis_index("head")
@@ -53,23 +53,17 @@
     for r in range(1, PEERS):
         pl.semaphore_signal(barrier, inc=1, device_id=(c, to_peer(r)), device_id_type=MESH)
     pl.semaphore_signal(barrier, inc=1, device_id=(sibling, h), device_id_type=MESH)
-    @pl.when(c >= 2)
-    def _():
-        for j in range(PEERS):
-            pl.semaphore_signal(barrier, inc=1, device_id=(c - 2, j), device_id_type=MESH)
-
-    @pl.when(c < N_CTX - 2)
-    def _():
-        for j in range(PEERS):
-            pl.semaphore_signal(barrier, inc=1, device_id=(c + 2, j), device_id_type=MESH)
-
-    @pl.when(c >= 4)
-    def _():
-        pl.semaphore_signal(barrier, inc=1, device_id=(c - 4, h), device_id_type=MESH)
-
-    @pl.when(c < N_CTX - 4)
-    def _():
-        pl.semaphore_signal(barrier, inc=1, device_id=(c + 4, h), device_id_type=MESH)
+
+    for step in (2, 4):
+        @pl.when(c >= step)
+        def _():
+            for j in range(PEERS):
+                pl.semaphore_signal(barrier, inc=1, device_id=(c - step, j), device_id_type=MESH)
+
+        @pl.when(c < N_CTX - step)
+        def _():
+            for j in range(PEERS):
+                pl.semaphore_signal(barrier, inc=1, device_id=(c + step, j), device_id_type=MESH)
 
     fetches = [
         pltpu.make_async_copy(source, target, in_sem.at[number])
@@ -120,8 +114,8 @@
     pl.semaphore_wait(
         barrier,
         PEERS
-        + PEERS * (c >= 2).astype(jnp.int32) + (c >= 4).astype(jnp.int32)
-        + PEERS * (c < N_CTX - 2).astype(jnp.int32) + (c < N_CTX - 4).astype(jnp.int32),
+        + PEERS * ((c >= 2).astype(jnp.int32) + (c >= 4).astype(jnp.int32))
+        + PEERS * ((c < N_CTX - 2).astype(jnp.int32) + (c < N_CTX - 4).astype(jnp.int32)),
     )
 
     my_rows = pl.ds(pl.multiple_of(h * ROWS, ROWS), ROWS)
@@ -135,27 +129,31 @@
         )
         kv_copies[r].start()
 
-    after2 = lax.rem(c + 2, N_CTX)
-    a_copies = [
-        pltpu.make_async_remote_copy(
-            src_ref=kvs.at[j], dst_ref=kvr2.at[my_rows],
-            send_sem=a_send.at[j], recv_sem=a_recv.at[h],
-            device_id=(after2, j), device_id_type=MESH,
+    def code_copies(step):
+        place, after = step // 2 - 1, lax.rem(c + step, N_CTX)
+        copies = [
+            pltpu.make_async_remote_copy(
+                src_ref=kvs.at[j], dst_ref=kvr2.at[place, my_rows],
+                send_sem=a_send.at[place, j], recv_sem=a_recv.at[place, h],
+                device_id=(after, j), device_id_type=MESH,
+            )
+            for j in range(PEERS)
+        ]
+        copies.append(
+            pltpu.make_async_remote_copy(
+                src_ref=kvb.at[0, META:KV_ROWS], dst_ref=kvb.at[step, META:KV_ROWS],
+                send_sem=a_send.at[place, PEERS], recv_sem=a_recv.at[place, PEERS],
+                device_id=(after, h), device_id_type=MESH,
+            )
         )
-        for j in range(PEERS)
-    ]
-    a_copies.append(
-        pltpu.make_async_remote_copy(
-            src_ref=kvb.at[0, META:KV_ROWS], dst_ref=kvb.at[2, META:KV_ROWS],
-            send_sem=a_send.at[PEERS], recv_sem=a_recv.at[PEERS],
-            device_id=(after2, h), device_id_type=MESH,
-        )
-    )
-
-    @pl.when(c < N_CTX - 2)
-    def _():
-        for copy in a_copies:
-            copy.start()
+        return copies
+
+    a_copies = {step: code_copies(step) for step in (2, 4)}
+    for step in (2, 4):
+        @pl.when(c < N_CTX - step)
+        def _():
+            for copy in a_copies[step]:
+                copy.start()
 
     def q_copy(r):
         peer = to_peer(r)
@@ -202,16 +200,8 @@
             device_id=(target, h), device_id_type=MESH,
         )
 
-    c_copies = {
-        1: c_copy(2 * core, 1, sibling),
-        3: c_copy(2 + 2 * core, 3, sibling),
-        4: c_copy(0, 4, lax.rem(c + 4, N_CTX)),
-    }
+    c_copies = {1: c_copy(2 * core, 1, sibling), 3: c_copy(2 + 2 * core, 3, sibling)}
     rotate(kvr, 0)
-
-    @pl.when(c < N_CTX - 4)
-    def _():
-        c_copies[4].start()
 
     @pl.when(core == 0)
     def _():
@@ -221,24 +211,24 @@
         q_copies[r].start()
     key_spans(0)
 
-    @pl.when(c >= 2)
-    def _():
-        for j in range(PEERS):
-            pltpu.make_async_remote_copy(
-                src_ref=kvs.at[0], dst_ref=kvr2.at[j * ROWS:(j + 1) * ROWS],
-                send_sem=a_send.at[0], recv_sem=a_recv.at[j],
-                device_id=(after2, h), device_id_type=MESH,
-            ).wait_recv()
-        a_copies[PEERS].wait_recv()
-        rotate(kvr2, 2)
-
-    @pl.when(c < 2)
-    def _():
-        kvb[2] = jnp.zeros((KV_ROWS, D), BF16)
-
-    @pl.when(c < 4)
-    def _():
-        kvb[4] = jnp.zeros((KV_ROWS, D), BF16)
+    def receive(step):
+        @pl.when(c >= step)
+        def _():
+            place = step // 2 - 1
+            for j in range(PEERS):
+                pltpu.make_async_remote_copy(
+                    src_ref=kvs.at[0], dst_ref=kvr2.at[place, j * ROWS:(j + 1) * ROWS],
+                    send_sem=a_send.at[place, 0], recv_sem=a_recv.at[place, j],
+                    device_id=(lax.rem(c + step, N_CTX), h), device_id_type=MESH,
+                ).wait_recv()
+            a_copies[step][PEERS].wait_recv()
+            rotate(kvr2.at[place], step)
+
+        @pl.when(c < step)
+        def _():
+            kvb[step] = jnp.zeros((KV_ROWS, D), BF16)
+
+    receive(2)
 
     @pl.when(core == 0)
     def _():
@@ -249,10 +239,7 @@
         c_copies[1].start()
 
     key_spans(2)
-
-    @pl.when(c >= 4)
-    def _():
-        c_copies[4].wait_recv()
+    receive(4)
 
     @pl.when(core == 1)
     def _():
@@ -328,10 +315,13 @@
         for g in range(2):
             attended = accum[g] * (1.0 / jnp.sum(total[g], axis=0, keepdims=True))
             attended = attended.T.astype(BF16)
-            rows = pl.ds(pl.multiple_of(p * ROWS, ROWS), ROWS)
             for i in range(GROUP // 2):
                 column = (g * GROUP // 2 + i) * D
-                out_ref[rows, column:column + D] = attended[i * ROWS:(i + 1) * ROWS]
+                ob[p, :, column:column + D] = attended[i * ROWS:(i + 1) * ROWS]
+
+    def out_copy(p):
+        rows = pl.ds(pl.multiple_of(p * ROWS, ROWS), ROWS)
+        return pltpu.make_async_copy(ob.at[p], out_hbm.at[rows], out_sem.at[p])
 
     def body(i, carry):
         turn, rx = lax.rem(i, 4), i // 4
@@ -358,34 +348,47 @@
         def _():
             attend(p, BLOCK, half)
 
+        out_copy(p).start()
         return carry
 
     lax.fori_loop(0, PEERS, body, 0)
 
+    for p in range(PEERS):
+        out_copy(p).wait()
     for r in range(1, PEERS):
         kv_copies[r].wait_send()
         q_copies[r].wait_send()
     for step in (1, 3):
         c_copies[step].wait_send()
 
-    @pl.when(c < N_CTX - 2)
-    def _():
-        for copy in a_copies:
-            copy.wait_send()
-
-    @pl.when(c < N_CTX - 4)
-    def _():
-        c_copies[4].wait_send()
+    for step in (2, 4):
+        @pl.when(c < N_CTX - step)
+        def _():
+            for copy in a_copies[step]:
+                copy.wait_send()
+
+
+def hand_over(source, target, held, in_sem, out_sem):
+    rows = [pl.ds(p * ROWS, ROWS) for p in range(PEERS)]
+    arrive = [pltpu.make_async_copy(source.at[r], held.at[r], in_sem.at[n]) for n, r in enumerate(rows)]
+    leave = [pltpu.make_async_copy(held.at[r], target.at[r], out_sem.at[n]) for n, r in enumerate(rows)]
+    for copy in arrive:
+        copy.start()
+    for n in range(PEERS):
+        arrive[n].wait()
+        leave[n].start()
+    for copy in leave:
+        copy.wait()
 
 
 def per_device(queries, key_codes, value_codes, key_exponents, value_exponents, trace_ids):
     hbm = pl.BlockSpec(memory_space=pl.ANY)
     dma = pltpu.SemaphoreType.DMA
-    return pl.pallas_call(
+    attended = pl.pallas_call(
         kernel,
         out_shape=jax.ShapeDtypeStruct((BLOCK, GROUP * D), BF16),
         in_specs=[hbm] * 6,
-        out_specs=pl.BlockSpec(memory_space=pltpu.VMEM),
+        out_specs=hbm,
         scratch_shapes=[
             pltpu.VMEM((ROWS, PEERS * GROUP * D), BF16),
             pltpu.VMEM((ROWS, PEERS * D), BF16),
@@ -395,14 +398,15 @@
             pltpu.VMEM((1, BLOCK), jnp.int32),
             pltpu.VMEM((PEERS, ROWS, 2 * D), BF16),
             pltpu.VMEM((BLOCK, 2 * D), BF16),
-            pltpu.VMEM((BLOCK, 2 * D), BF16),
+            pltpu.VMEM((2, BLOCK, 2 * D), BF16),
             pltpu.VMEM((STEPS + 1, KV_ROWS, D), BF16),
             pltpu.VMEM((PEERS, ROWS, GROUP * D), BF16),
             pltpu.VMEM((BLOCK, D), BF16),
             pltpu.VMEM((STEPS + 1, BLOCK, D), BF16),
             pltpu.VMEM((2, BLOCK, BLOCK), F32),
+            pltpu.VMEM((PEERS, ROWS, GROUP * D), BF16),
             dma((7,)), dma((PEERS,)), dma((PEERS,)), dma((PEERS,)), dma((PEERS,)),
-            dma((PEERS + 1,)), dma((PEERS + 1,)), dma((STEPS + 1,)), dma((STEPS + 1,)),
+            dma((2, PEERS + 1)), dma((2, PEERS + 1)), dma((STEPS + 1,)), dma((STEPS + 1,)), dma((PEERS,)),
         ],
         compiler_params=pltpu.CompilerParams(
             collective_id=0, has_side_effects=True, vmem_limit_bytes=62 * 1024 * 1024
@@ -411,6 +415,14 @@
     )(
         queries, key_codes, value_codes, key_exponents.T, value_exponents.T, trace_ids.reshape(1, BLOCK)
     )
+    return pl.pallas_call(
+        hand_over,
+        out_shape=jax.ShapeDtypeStruct((BLOCK, GROUP * D), BF16),
+        in_specs=[hbm],
+        out_specs=hbm,
+        scratch_shapes=[pltpu.VMEM((BLOCK, GROUP * D), BF16), dma((PEERS,)), dma((PEERS,))],
+        compiler_params=pltpu.CompilerParams(vmem_limit_bytes=62 * 1024 * 1024),
+    )(attended)
 
 
 def solution(mesh):

time: 39.8 us -> 43.5 us (1.093)
  the two profiles are of different devices: /device:TPU:224 before, /device:TPU:184 now
where the time goes in v6:
time: 43.5 us; the launch traced here: 43.4 us
  Pallas kernels  43.4 us (100%)
    pallas_call x1, Pallas kernels, per_device(): pl.pallas_call(kernel, out_shape=jax.ShapeDtypeStruct((BLOCK, GROUP * D),...  41.3 us
    pallas_call x1, Pallas kernels, per_device(): pl.pallas_call(hand_over, out_shape=jax.ShapeDtypeStruct((BLOCK, GROUP *...  2.09 us

profile of v6, /device:TPU:184, one launch (start us, length us, event | category | flops | bytes accessed | tf_op | source)
XLA Modules:
  0.0 43.4 jit_solution(4252414012214272167)
XLA Ops:
  0.0 41.3 %shard_map.64.source = bf16[512,1024]{1,0:T(8,128)(2,1)} custom-call(bf16[64,8192]{1,0:T(8,128)(2,1)} %q_hbm.1, bf16[64,1024]{1,0:T(8,128)(2,1)} %kc_hbm.1, bf16[64,1024]{1,0:T(8,128)(2,1)} %vc_hbm.1, s32[8,64]{1,0:T(8,128)} %bitcast.3, s32[8,64]{1,0:T(8,128)} %bitcast.4, s32[1,512]{1,0:T(1,128)} %bitcast.5), custom_call_target="tpu_custom_call" | custom-call | flops 8999999488 | bytes 4000000 | tf_op jit(solution)/shard_map/pallas_call | solution.py:387
  41.3 2.1 %shard_map.65 = bf16[512,1024]{1,0:T(8,128)(2,1)} custom-call(bf16[512,1024]{1,0:T(8,128)(2,1)} %shard_map.64.source), custom_call_target="tpu_custom_call" | custom-call | tf_op jit(solution)/shard_map/pallas_call | solution.py:418

commit v7 on v1

--- a/solution.py
+++ b/solution.py
@@ -33,10 +33,10 @@
 
 
 def kernel(
-    q_hbm, kc_hbm, vc_hbm, ke_hbm, ve_hbm, ids_hbm, out_ref,
+    q_hbm, kc_hbm, vc_hbm, ke_hbm, ve_hbm, ids_hbm, out_hbm,
     q_ref, kc_ref, vc_ref, ke_ref, ve_ref, ids_ref,
-    kvs, kvr, kvr2, kvb, qb, aug_q, aug_k, s_buf,
-    in_sem, kv_send, kv_recv, q_send, q_recv, a_send, a_recv, c_send, c_recv,
+    kvs, kvr, kvr2, kvb, qb, aug_q, aug_k, s_buf, ob,
+    in_sem, kv_send, kv_recv, q_send, q_recv, a_send, a_recv, c_send, c_recv, out_sem,
 ):
     c = lax.axis_index("ctx")
     h = lax.axis_index("head")
@@ -53,6 +53,7 @@
     for r in range(1, PEERS):
         pl.semaphore_signal(barrier, inc=1, device_id=(c, to_peer(r)), device_id_type=MESH)
     pl.semaphore_signal(barrier, inc=1, device_id=(sibling, h), device_id_type=MESH)
+
     @pl.when(c >= 2)
     def _():
         for j in range(PEERS):
@@ -135,22 +136,26 @@
         )
         kv_copies[r].start()
 
-    after2 = lax.rem(c + 2, N_CTX)
-    a_copies = [
-        pltpu.make_async_remote_copy(
-            src_ref=kvs.at[j], dst_ref=kvr2.at[my_rows],
-            send_sem=a_send.at[j], recv_sem=a_recv.at[h],
-            device_id=(after2, j), device_id_type=MESH,
+    def code_copies(step):
+        after = lax.rem(c + step, N_CTX)
+        copies = [
+            pltpu.make_async_remote_copy(
+                src_ref=kvs.at[j], dst_ref=kvr2.at[my_rows],
+                send_sem=a_send.at[j], recv_sem=a_recv.at[h],
+                device_id=(after, j), device_id_type=MESH,
+            )
+            for j in range(PEERS)
+        ]
+        copies.append(
+            pltpu.make_async_remote_copy(
+                src_ref=kvb.at[0, META:KV_ROWS], dst_ref=kvb.at[step, META:KV_ROWS],
+                send_sem=a_send.at[PEERS], recv_sem=a_recv.at[PEERS],
+                device_id=(after, h), device_id_type=MESH,
+            )
         )
-        for j in range(PEERS)
-    ]
-    a_copies.append(
-        pltpu.make_async_remote_copy(
-            src_ref=kvb.at[0, META:KV_ROWS], dst_ref=kvb.at[2, META:KV_ROWS],
-            send_sem=a_send.at[PEERS], recv_sem=a_recv.at[PEERS],
-            device_id=(after2, h), device_id_type=MESH,
-        )
-    )
+        return copies
+
+    a_copies = code_copies(2)
 
     @pl.when(c < N_CTX - 2)
     def _():
@@ -168,8 +173,6 @@
     q_copies = {r: q_copy(r) for r in range(1, PEERS)}
     fetches[5].wait()
     own_q.start()
-    for r in (2, 6, 4):
-        q_copies[r].start()
     kvr[my_rows] = kvs[h]
 
     token = iota((BLOCK, D), 0).astype(F32)
@@ -217,7 +220,7 @@
     def _():
         c_copies[1].start()
 
-    for r in (1, 3, 7, 5):
+    for r in (2, 6, 1, 4, 3, 7, 5):
         q_copies[r].start()
     key_spans(0)
 
@@ -227,7 +230,7 @@
             pltpu.make_async_remote_copy(
                 src_ref=kvs.at[0], dst_ref=kvr2.at[j * ROWS:(j + 1) * ROWS],
                 send_sem=a_send.at[0], recv_sem=a_recv.at[j],
-                device_id=(after2, h), device_id_type=MESH,
+                device_id=(lax.rem(c + 2, N_CTX), h), device_id_type=MESH,
             ).wait_recv()
         a_copies[PEERS].wait_recv()
         rotate(kvr2, 2)
@@ -328,10 +331,13 @@
         for g in range(2):
             attended = accum[g] * (1.0 / jnp.sum(total[g], axis=0, keepdims=True))
             attended = attended.T.astype(BF16)
-            rows = pl.ds(pl.multiple_of(p * ROWS, ROWS), ROWS)
             for i in range(GROUP // 2):
                 column = (g * GROUP // 2 + i) * D
-                out_ref[rows, column:column + D] = attended[i * ROWS:(i + 1) * ROWS]
+                ob[p, :, column:column + D] = attended[i * ROWS:(i + 1) * ROWS]
+
+    def out_copy(p):
+        rows = pl.ds(pl.multiple_of(p * ROWS, ROWS), ROWS)
+        return pltpu.make_async_copy(ob.at[p], out_hbm.at[rows], out_sem.at[p])
 
     def body(i, carry):
         turn, rx = lax.rem(i, 4), i // 4
@@ -358,10 +364,13 @@
         def _():
             attend(p, BLOCK, half)
 
+        out_copy(p).start()
         return carry
 
     lax.fori_loop(0, PEERS, body, 0)
 
+    for p in range(PEERS):
+        out_copy(p).wait()
     for r in range(1, PEERS):
         kv_copies[r].wait_send()
         q_copies[r].wait_send()
@@ -378,14 +387,27 @@
         c_copies[4].wait_send()
 
 
+def hand_over(source, target, held, in_sem, out_sem):
+    rows = [pl.ds(p * ROWS, ROWS) for p in range(PEERS)]
+    arrive = [pltpu.make_async_copy(source.at[r], held.at[r], in_sem.at[n]) for n, r in enumerate(rows)]
+    leave = [pltpu.make_async_copy(held.at[r], target.at[r], out_sem.at[n]) for n, r in enumerate(rows)]
+    for copy in arrive:
+        copy.start()
+    for n in range(PEERS):
+        arrive[n].wait()
+        leave[n].start()
+    for copy in leave:
+        copy.wait()
+
+
 def per_device(queries, key_codes, value_codes, key_exponents, value_exponents, trace_ids):
     hbm = pl.BlockSpec(memory_space=pl.ANY)
     dma = pltpu.SemaphoreType.DMA
-    return pl.pallas_call(
+    attended = pl.pallas_call(
         kernel,
         out_shape=jax.ShapeDtypeStruct((BLOCK, GROUP * D), BF16),
         in_specs=[hbm] * 6,
-        out_specs=pl.BlockSpec(memory_space=pltpu.VMEM),
+        out_specs=hbm,
         scratch_shapes=[
             pltpu.VMEM((ROWS, PEERS * GROUP * D), BF16),
             pltpu.VMEM((ROWS, PEERS * D), BF16),
@@ -401,8 +423,9 @@
             pltpu.VMEM((BLOCK, D), BF16),
             pltpu.VMEM((STEPS + 1, BLOCK, D), BF16),
             pltpu.VMEM((2, BLOCK, BLOCK), F32),
+            pltpu.VMEM((PEERS, ROWS, GROUP * D), BF16),
             dma((7,)), dma((PEERS,)), dma((PEERS,)), dma((PEERS,)), dma((PEERS,)),
-            dma((PEERS + 1,)), dma((PEERS + 1,)), dma((STEPS + 1,)), dma((STEPS + 1,)),
+            dma((PEERS + 1,)), dma((PEERS + 1,)), dma((STEPS + 1,)), dma((STEPS + 1,)), dma((PEERS,)),
         ],
         compiler_params=pltpu.CompilerParams(
             collective_id=0, has_side_effects=True, vmem_limit_bytes=62 * 1024 * 1024
@@ -411,6 +434,14 @@
     )(
         queries, key_codes, value_codes, key_exponents.T, value_exponents.T, trace_ids.reshape(1, BLOCK)
     )
+    return pl.pallas_call(
+        hand_over,
+        out_shape=jax.ShapeDtypeStruct((BLOCK, GROUP * D), BF16),
+        in_specs=[hbm],
+        out_specs=hbm,
+        scratch_shapes=[pltpu.VMEM((BLOCK, GROUP * D), BF16), dma((PEERS,)), dma((PEERS,))],
+        compiler_params=pltpu.CompilerParams(vmem_limit_bytes=62 * 1024 * 1024),
+    )(attended)
 
 
 def solution(mesh):

time: 39.8 us -> 43.9 us (1.10)
  the two profiles are of different devices: /device:TPU:224 before, /device:TPU:100 now
where the time goes in v7:
time: 43.9 us; the launch traced here: 43.8 us
  Pallas kernels  43.8 us (100%)
    pallas_call x1, Pallas kernels, per_device(): pl.pallas_call(kernel, out_shape=jax.ShapeDtypeStruct((BLOCK, GROUP * D),...  41.7 us
    pallas_call x1, Pallas kernels, per_device(): pl.pallas_call(hand_over, out_shape=jax.ShapeDtypeStruct((BLOCK, GROUP *...  2.09 us

profile of v7, /device:TPU:100, one launch (start us, length us, event | category | flops | bytes accessed | tf_op | source)
XLA Modules:
  0.0 43.8 jit_solution(17909231726972543065)
XLA Ops:
  0.0 41.7 %shard_map.64.source = bf16[512,1024]{1,0:T(8,128)(2,1)} custom-call(bf16[64,8192]{1,0:T(8,128)(2,1)} %q_hbm.1, bf16[64,1024]{1,0:T(8,128)(2,1)} %kc_hbm.1, bf16[64,1024]{1,0:T(8,128)(2,1)} %vc_hbm.1, s32[8,64]{1,0:T(8,128)} %bitcast.3, s32[8,64]{1,0:T(8,128)} %bitcast.4, s32[1,512]{1,0:T(1,128)} %bitcast.5), custom_call_target="tpu_custom_call" | custom-call | flops 8999999488 | bytes 4000000 | tf_op jit(solution)/shard_map/pallas_call | solution.py:406
  41.7 2.1 %shard_map.65 = bf16[512,1024]{1,0:T(8,128)(2,1)} custom-call(bf16[512,1024]{1,0:T(8,128)(2,1)} %shard_map.64.source), custom_call_target="tpu_custom_call" | custom-call | tf_op jit(solution)/shard_map/pallas_call | solution.py:437

commit v8 on v3

--- a/solution.py
+++ b/solution.py
@@ -33,10 +33,10 @@
 
 
 def kernel(
-    q_hbm, kc_hbm, vc_hbm, ke_hbm, ve_hbm, ids_hbm, out_ref,
+    q_hbm, kc_hbm, vc_hbm, ke_hbm, ve_hbm, ids_hbm, out_hbm,
     q_ref, kc_ref, vc_ref, ke_ref, ve_ref, ids_ref,
-    kvs, kvr, kvr2, kvb, qb, qt, aug_q, aug_k, s_buf, top_s, m_s, l_s, o_s,
-    in_sem, kv_send, kv_recv, q_send, q_recv, a_send, a_recv, c_send, c_recv,
+    kvs, kvr, kvr2, kvb, qb, qt, aug_q, aug_k, s_buf, top_s, m_s, l_s, o_s, ob,
+    in_sem, kv_send, kv_recv, q_send, q_recv, a_send, a_recv, c_send, c_recv, out_sem,
 ):
     c = lax.axis_index("ctx")
     h = lax.axis_index("head")
@@ -175,7 +175,7 @@
     q_copies = {r: q_copy(r) for r in range(1, PEERS)}
     fetches[5].wait()
     own_q.start()
-    for r in (1, 2, 3, 4, 5):
+    for r in (1, 4, 5):
         q_copies[r].start()
     kvr[my_rows] = kvs[h]
 
@@ -224,7 +224,7 @@
     def _():
         c_copies[1].start()
 
-    for r in (6, 7):
+    for r in (2, 3, 6, 7):
         q_copies[r].start()
     key_spans(0)
 
@@ -302,6 +302,10 @@
     def values_of(d, k):
         parts = [kvb[d, BLOCK + part * D:BLOCK + (part + 1) * D] for part in range(k // D, (k + half) // D)]
         return jnp.concatenate(parts, axis=1)
+
+    def out_copy(p):
+        rows = pl.ds(pl.multiple_of(p * ROWS, ROWS), ROWS)
+        return pltpu.make_async_copy(ob.at[p], out_hbm.at[rows], out_sem.at[p])
 
     def pieces(span):
         return [(k, g) for g in range(2) for k in range(*span, half)]
@@ -340,7 +344,6 @@
                 total[g] = sums if total[g] is None else total[g] + sums
                 accum[g] = product if accum[g] is None else accum[g] + product
             top = next_top
-        rows = pl.ds(pl.multiple_of(p * ROWS, ROWS), ROWS)
         for g in range(2):
             top_s[:, rows_of[g]] = top[g]
             if steps[-1] < STEPS:
@@ -350,7 +353,9 @@
             attended = attended.T.astype(BF16)
             for member in range(GROUP // 2):
                 column = (g * GROUP // 2 + member) * D
-                out_ref[rows, column:column + D] = attended[member * ROWS:(member + 1) * ROWS]
+                ob[p, :, column:column + D] = attended[member * ROWS:(member + 1) * ROWS]
+        if steps[-1] == STEPS:
+            out_copy(p).start()
 
     def await_queries(turn, n):
         p = partner(turn, n)
@@ -408,6 +413,8 @@
     await_queries(1, 0)
     either(jnp.logical_not(own_early), 1, (0, 1, 2, 3, 4), {0: 0, 1: 1, 2: 0, 3: 1, 4: 2})
 
+    for p in range(PEERS):
+        out_copy(p).wait()
     for r in range(1, PEERS):
         kv_copies[r].wait_send()
         q_copies[r].wait_send()
@@ -424,14 +431,27 @@
         c_copies[4].wait_send()
 
 
+def hand_over(source, target, held, in_sem, out_sem):
+    rows = [pl.ds(p * ROWS, ROWS) for p in range(PEERS)]
+    arrive = [pltpu.make_async_copy(source.at[r], held.at[r], in_sem.at[n]) for n, r in enumerate(rows)]
+    leave = [pltpu.make_async_copy(held.at[r], target.at[r], out_sem.at[n]) for n, r in enumerate(rows)]
+    for copy in arrive:
+        copy.start()
+    for n in range(PEERS):
+        arrive[n].wait()
+        leave[n].start()
+    for copy in leave:
+        copy.wait()
+
+
 def per_device(queries, key_codes, value_codes, key_exponents, value_exponents, trace_ids):
     hbm = pl.BlockSpec(memory_space=pl.ANY)
     dma = pltpu.SemaphoreType.DMA
-    return pl.pallas_call(
+    attended = pl.pallas_call(
         kernel,
         out_shape=jax.ShapeDtypeStruct((BLOCK, GROUP * D), BF16),
         in_specs=[hbm] * 6,
-        out_specs=pl.BlockSpec(memory_space=pltpu.VMEM),
+        out_specs=hbm,
         scratch_shapes=[
             pltpu.VMEM((ROWS, PEERS * GROUP * D), BF16),
             pltpu.VMEM((ROWS, PEERS * D), BF16),
@@ -452,8 +472,9 @@
             pltpu.VMEM((4, 1, BLOCK), F32),
             pltpu.VMEM((4, 8, BLOCK), F32),
             pltpu.VMEM((4, D, BLOCK), F32),
+            pltpu.VMEM((PEERS, ROWS, GROUP * D), BF16),
             dma((7,)), dma((PEERS,)), dma((PEERS,)), dma((PEERS,)), dma((PEERS,)),
-            dma((PEERS + 1,)), dma((PEERS + 1,)), dma((STEPS + 1,)), dma((STEPS + 1,)),
+            dma((PEERS + 1,)), dma((PEERS + 1,)), dma((STEPS + 1,)), dma((STEPS + 1,)), dma((PEERS,)),
         ],
         compiler_params=pltpu.CompilerParams(
             collective_id=0, has_side_effects=True, vmem_limit_bytes=62 * 1024 * 1024
@@ -462,6 +483,14 @@
     )(
         queries, key_codes, value_codes, key_exponents.T, value_exponents.T, trace_ids.reshape(1, BLOCK)
     )
+    return pl.pallas_call(
+        hand_over,
+        out_shape=jax.ShapeDtypeStruct((BLOCK, GROUP * D), BF16),
+        in_specs=[hbm],
+        out_specs=hbm,
+        scratch_shapes=[pltpu.VMEM((BLOCK, GROUP * D), BF16), dma((PEERS,)), dma((PEERS,))],
+        compiler_params=pltpu.CompilerParams(vmem_limit_bytes=62 * 1024 * 1024),
+    )(attended)
 
 
 def solution(mesh):

time: 38.8 us -> 38.5 us (level)
  the two profiles are of different devices: /device:TPU:6 before, /device:TPU:100 now
where the time goes in v8:
time: 38.5 us; the launch traced here: 37.8 us
  Pallas kernels  37.8 us (98%)
    pallas_call x1, Pallas kernels, per_device(): pl.pallas_call(kernel, out_shape=jax.ShapeDtypeStruct((BLOCK, GROUP * D),...  35.7 us
    pallas_call x1, Pallas kernels, per_device(): pl.pallas_call(hand_over, out_shape=jax.ShapeDtypeStruct((BLOCK, GROUP *...  2.09 us

profile of v8, /device:TPU:100, one launch (start us, length us, event | category | flops | bytes accessed | tf_op | source)
XLA Modules:
  0.0 37.8 jit_solution(7023626426516811314)
XLA Ops:
  0.0 35.7 %shard_map.64.source = bf16[512,1024]{1,0:T(8,128)(2,1)} custom-call(bf16[64,8192]{1,0:T(8,128)(2,1)} %q_hbm.1, bf16[64,1024]{1,0:T(8,128)(2,1)} %kc_hbm.1, bf16[64,1024]{1,0:T(8,128)(2,1)} %vc_hbm.1, s32[8,64]{1,0:T(8,128)} %bitcast.3, s32[8,64]{1,0:T(8,128)} %bitcast.4, s32[1,512]{1,0:T(1,128)} %bitcast.5), custom_call_target="tpu_custom_call" | custom-call | flops 8999999488 | bytes 4000000 | tf_op jit(solution)/shard_map/pallas_call | solution.py:450
  35.8 2.1 %shard_map.65 = bf16[512,1024]{1,0:T(8,128)(2,1)} custom-call(bf16[512,1024]{1,0:T(8,128)(2,1)} %shard_map.64.source), custom_call_target="tpu_custom_call" | custom-call | tf_op jit(solution)/shard_map/pallas_call | solution.py:486

commit v9 on v8

--- a/solution.py
+++ b/solution.py
@@ -376,7 +376,7 @@
 
         def body(n, carry):
             if steps == (0, 1, 2):
-                @pl.when((n == 2) & (core == 1))
+                @pl.when((n == 1) & (core == 1))
                 def _():
                     pass_on_farther_block()
 

time: 38.5 us -> 38.5 us (level)
  no operation moved by 1% of the time
where the time goes in v9:
time: 38.5 us; the launch traced here: 37.8 us
  Pallas kernels  37.8 us (98%)
    pallas_call x1, Pallas kernels, per_device(): pl.pallas_call(kernel, out_shape=jax.ShapeDtypeStruct((BLOCK, GROUP * D),...  35.7 us
    pallas_call x1, Pallas kernels, per_device(): pl.pallas_call(hand_over, out_shape=jax.ShapeDtypeStruct((BLOCK, GROUP *...  2.09 us

profile of v9, /device:TPU:100, one launch (start us, length us, event | category | flops | bytes accessed | tf_op | source)
XLA Modules:
  0.0 37.8 jit_solution(13172522906080175599)
XLA Ops:
  0.0 35.7 %shard_map.64.source = bf16[512,1024]{1,0:T(8,128)(2,1)} custom-call(bf16[64,8192]{1,0:T(8,128)(2,1)} %q_hbm.1, bf16[64,1024]{1,0:T(8,128)(2,1)} %kc_hbm.1, bf16[64,1024]{1,0:T(8,128)(2,1)} %vc_hbm.1, s32[8,64]{1,0:T(8,128)} %bitcast.3, s32[8,64]{1,0:T(8,128)} %bitcast.4, s32[1,512]{1,0:T(1,128)} %bitcast.5), custom_call_target="tpu_custom_call" | custom-call | flops 8999999488 | bytes 4000000 | tf_op jit(solution)/shard_map/pallas_call | solution.py:450
  35.8 2.1 %shard_map.65 = bf16[512,1024]{1,0:T(8,128)(2,1)} custom-call(bf16[512,1024]{1,0:T(8,128)(2,1)} %shard_map.64.source), custom_call_target="tpu_custom_call" | custom-call | tf_op jit(solution)/shard_map/pallas_call | solution.py:486

commit v10 on v8

--- a/solution.py
+++ b/solution.py
@@ -224,8 +224,14 @@
     def _():
         c_copies[1].start()
 
-    for r in (2, 3, 6, 7):
+    for r in (2, 3):
         q_copies[r].start()
+
+    @pl.when(core == 0)
+    def _():
+        for r in (6, 7):
+            q_copies[r].start()
+
     key_spans(0)
 
     @pl.when(c >= 2)
@@ -254,6 +260,8 @@
     @pl.when(core == 1)
     def _():
         c_copies[1].start()
+        for r in (6, 7):
+            q_copies[r].start()
 
     key_spans(2)
     c_copies[1].wait_recv()

time: 38.5 us -> 38.5 us (level)
  no operation moved by 1% of the time
where the time goes in v10:
time: 38.5 us; the launch traced here: 37.8 us
  Pallas kernels  37.8 us (98%)
    pallas_call x1, Pallas kernels, per_device(): pl.pallas_call(kernel, out_shape=jax.ShapeDtypeStruct((BLOCK, GROUP * D),...  35.7 us
    pallas_call x1, Pallas kernels, per_device(): pl.pallas_call(hand_over, out_shape=jax.ShapeDtypeStruct((BLOCK, GROUP *...  2.09 us

profile of v10, /device:TPU:100, one launch (start us, length us, event | category | flops | bytes accessed | tf_op | source)
XLA Modules:
  0.0 37.8 jit_solution(18081892191852867533)
XLA Ops:
  0.0 35.7 %shard_map.64.source = bf16[512,1024]{1,0:T(8,128)(2,1)} custom-call(bf16[64,8192]{1,0:T(8,128)(2,1)} %q_hbm.1, bf16[64,1024]{1,0:T(8,128)(2,1)} %kc_hbm.1, bf16[64,1024]{1,0:T(8,128)(2,1)} %vc_hbm.1, s32[8,64]{1,0:T(8,128)} %bitcast.3, s32[8,64]{1,0:T(8,128)} %bitcast.4, s32[1,512]{1,0:T(1,128)} %bitcast.5), custom_call_target="tpu_custom_call" | custom-call | flops 8999999488 | bytes 4000000 | tf_op jit(solution)/shard_map/pallas_call | solution.py:458
  35.8 2.1 %shard_map.65 = bf16[512,1024]{1,0:T(8,128)(2,1)} custom-call(bf16[512,1024]{1,0:T(8,128)(2,1)} %shard_map.64.source), custom_call_target="tpu_custom_call" | custom-call | tf_op jit(solution)/shard_map/pallas_call | solution.py:494

commit v11 on v8

--- a/solution.py
+++ b/solution.py
@@ -175,7 +175,7 @@
     q_copies = {r: q_copy(r) for r in range(1, PEERS)}
     fetches[5].wait()
     own_q.start()
-    for r in (1, 4, 5):
+    for r in (1,):
         q_copies[r].start()
     kvr[my_rows] = kvs[h]
 
@@ -224,7 +224,7 @@
     def _():
         c_copies[1].start()
 
-    for r in (2, 3, 6, 7):
+    for r in (2, 3, 4, 6, 5, 7):
         q_copies[r].start()
     key_spans(0)
 

time: 38.5 us -> 38.5 us (level)
  no operation moved by 1% of the time
where the time goes in v11:
time: 38.5 us; the launch traced here: 37.9 us
  Pallas kernels  37.8 us (98%)
    pallas_call x1, Pallas kernels, per_device(): pl.pallas_call(kernel, out_shape=jax.ShapeDtypeStruct((BLOCK, GROUP * D),...  35.8 us
    pallas_call x1, Pallas kernels, per_device(): pl.pallas_call(hand_over, out_shape=jax.ShapeDtypeStruct((BLOCK, GROUP *...  2.09 us

profile of v11, /device:TPU:100, one launch (start us, length us, event | category | flops | bytes accessed | tf_op | source)
XLA Modules:
  0.0 37.9 jit_solution(3826462327718259372)
XLA Ops:
  0.0 35.8 %shard_map.64.source = bf16[512,1024]{1,0:T(8,128)(2,1)} custom-call(bf16[64,8192]{1,0:T(8,128)(2,1)} %q_hbm.1, bf16[64,1024]{1,0:T(8,128)(2,1)} %kc_hbm.1, bf16[64,1024]{1,0:T(8,128)(2,1)} %vc_hbm.1, s32[8,64]{1,0:T(8,128)} %bitcast.3, s32[8,64]{1,0:T(8,128)} %bitcast.4, s32[1,512]{1,0:T(1,128)} %bitcast.5), custom_call_target="tpu_custom_call" | custom-call | flops 8999999488 | bytes 4000000 | tf_op jit(solution)/shard_map/pallas_call | solution.py:450
  35.8 2.1 %shard_map.65 = bf16[512,1024]{1,0:T(8,128)(2,1)} custom-call(bf16[512,1024]{1,0:T(8,128)(2,1)} %shard_map.64.source), custom_call_target="tpu_custom_call" | custom-call | tf_op jit(solution)/shard_map/pallas_call | solution.py:486
